TPU v7x, 128 devices: a whole 4x4x4 slice. The times are simulated.
128 devices in a mesh: stn: 16 (over y, x), chan: 4 (over z), beam: 2 (over core).
Axes of the slice: x: 4, y: 4, z: 4, core: 2. Of those that a mesh axis runs over, the one named last changes fastest.
Arguments:
- volts: bfloat16 [2, 512, 12, 9216], P(None, 'stn', 'chan', 'beam'), may hold values from -6 to 6
- taps: float32 [16, 256], replicated, may hold values from -1.5 to 1.5
- delays: int32 [128, 512], P(None, 'stn'), may hold values from 0 to 1023
- station_sub: int32 [512], P('stn'), may hold values from 0 to 3
- beam_sub: int32 [128], replicated, may hold values from 0 to 3
Outputs:
- beams: float32 [128, 2, 12, 48, 256], P(('stn', 'chan', 'beam'))
All inputs are finite; a program needn't handle non-finite values.
Results may differ from a plain program's by a relative error of at most 0.014.
Values may be sent and summed in bfloat16 or wider, within the bound.
No kernel may reach another device: no remote copies, remote signals or barrier semaphores. Data moves between devices by JAX's collectives and lax.ppermute only.
A program may use at most 192 MiB of HBM per device.

v0:
```python
import math

import jax
import jax.numpy as jnp
from jax import lax
from jax.sharding import PartitionSpec as P

SUBARRAYS = 4


def shifted(block, axis, distance):
    devices = range(lax.axis_size(axis))
    route = [(i - distance, i) for i in devices if i - distance in devices]
    return lax.ppermute(block, axis, route)


def filter_frames(extended, taps, frame_count):
    tap_count, fine = taps.shape
    hop = 3 * fine // 4
    groups = frame_count // 4
    rows = groups + (tap_count + 2) // 3
    shape = extended.shape
    needed = 3 * hop + 3 * rows * fine
    padding = max(0, needed - shape[-1])
    padded = jnp.concatenate(
        [extended, jnp.zeros(shape[:-1] + (padding,), extended.dtype)], axis=-1
    )
    streams = []
    for phase in range(4):
        start = phase * hop
        piece = lax.slice_in_dim(padded, start, start + 3 * rows * fine, 1, len(shape) - 1)
        streams.append(piece.reshape(shape[:-1] + (rows, 3, fine)))
    stacked = jnp.stack(streams, axis=-2)
    axis = len(shape) - 1
    total = None
    for tap in range(tap_count):
        lead = tap // 3
        inner = tap % 3
        window = lax.slice_in_dim(stacked, lead, lead + groups, 1, axis)[..., inner, :, :].astype(
            jnp.float32
        )
        term = taps[tap] * window
        total = term if total is None else total + term
    return total.reshape(shape[:-1] + (frame_count, fine)).astype(jnp.bfloat16)


def dft_tables(fine):
    index = jnp.arange(fine, dtype=jnp.int32)
    product = index[:, None] * index[None, :] % fine
    angle = 2.0 * jnp.pi * product.astype(jnp.float32) / fine
    scale = 1.0 / math.sqrt(fine)
    return (
        (jnp.cos(angle) * scale).astype(jnp.bfloat16),
        (jnp.sin(angle) * scale).astype(jnp.bfloat16),
    )


def channelize(filtered, frame_start, hop):
    fine = filtered.shape[-1]
    cosine, sine = dft_tables(fine)
    spec_re = jnp.einsum(
        "...j,jk->...k", filtered[0], cosine, preferred_element_type=jnp.float32
    ) + jnp.einsum("...j,jk->...k", filtered[1], sine, preferred_element_type=jnp.float32)
    spec_im = jnp.einsum(
        "...j,jk->...k", filtered[1], cosine, preferred_element_type=jnp.float32
    ) - jnp.einsum("...j,jk->...k", filtered[0], sine, preferred_element_type=jnp.float32)
    frame_count = filtered.shape[-2]
    frame_index = frame_start + jnp.arange(frame_count, dtype=jnp.int32)
    fine_index = jnp.arange(fine, dtype=jnp.int32)
    turn = fine_index[None, :] * hop % fine * frame_index[:, None] % fine
    rot = 2.0 * jnp.pi * turn.astype(jnp.float32) / fine
    cos_rot = jnp.cos(rot)
    sin_rot = jnp.sin(rot)
    out_re = spec_re * cos_rot + spec_im * sin_rot
    out_im = spec_im * cos_rot - spec_re * sin_rot
    return jnp.stack([out_re, out_im]).astype(jnp.bfloat16)


def steering_band(
    delay_rows, beam_subs, station_subs, chan_start, chan_count, fine, width, amplitude
):
    fine_index = jnp.arange(width, dtype=jnp.int32)
    chan_index = chan_start + jnp.arange(chan_count, dtype=jnp.int32)
    freq_index = chan_index[:, None] * fine + fine_index[None, :]
    turn = delay_rows[:, :, None, None] * freq_index[None, None, :, :] % 65536
    phase = 2.0 * jnp.pi * turn.astype(jnp.float32) / 65536.0
    member = (beam_subs[:, None] == station_subs[None, :]).astype(jnp.float32)[:, :, None, None]
    weight_re = (amplitude * member * jnp.cos(phase)).astype(jnp.bfloat16)
    weight_im = (-amplitude * member * jnp.sin(phase)).astype(jnp.bfloat16)
    return (weight_re, weight_im)


def complex_form(weight_re, weight_im, pieces):
    form = "bsck,scfk->bcfk"
    part_re = jnp.einsum(
        form, weight_re, pieces[0], preferred_element_type=jnp.float32
    ) - jnp.einsum(form, weight_im, pieces[1], preferred_element_type=jnp.float32)
    part_im = jnp.einsum(
        form, weight_re, pieces[1], preferred_element_type=jnp.float32
    ) + jnp.einsum(form, weight_im, pieces[0], preferred_element_type=jnp.float32)
    return jnp.stack([part_re, part_im], axis=1)


def body(volts, taps, delays, station_sub, beam_sub):
    tap_count, fine = taps.shape
    hop = 3 * fine // 4
    frames_dev = volts.shape[3] // hop
    chan_count = volts.shape[2]
    extra = tap_count * fine - hop
    tail = shifted(volts[:, :, :, :extra], "beam", -1)
    extended = jnp.concatenate([volts, tail], axis=3)
    chan_start = lax.axis_index("chan") * chan_count
    frame_start = lax.axis_index("beam") * frames_dev
    filtered = filter_frames(extended, taps, frames_dev)
    spectra = channelize(filtered, frame_start, hop)
    group_width = delays.shape[1]
    stn_size = lax.axis_size("stn")
    stations = group_width * stn_size
    amplitude = 1.0 / math.sqrt(stations // SUBARRAYS)
    weight_re, weight_im = steering_band(
        delays, beam_sub, station_sub, chan_start, chan_count, fine, fine, amplitude
    )
    summed = lax.psum_scatter(
        complex_form(weight_re, weight_im, spectra).astype(jnp.bfloat16),
        "stn",
        scatter_dimension=0,
        tiled=True,
    ).astype(jnp.float32)
    result = lax.all_to_all(
        lax.all_to_all(
            summed.astype(jnp.bfloat16), "chan", split_axis=0, concat_axis=2, tiled=True
        ),
        "beam",
        split_axis=0,
        concat_axis=3,
        tiled=True,
    ).astype(summed.dtype)
    return result


def solution(mesh):
    placed = (P(None, "stn", "chan", "beam"), P(), P(None, "stn"), P("stn"), P())
    return jax.shard_map(
        body,
        mesh=mesh,
        in_specs=placed,
        out_specs=P(("stn", "chan", "beam"), None, None, None, None),
        check_vma=False,
    )
```

profile of v0, /device:TPU:1, one launch (start us, length us, event | category | flops | bytes accessed | tf_op | source)
XLA Modules:
  0.0 608.0 jit_solution(12361677105210901414)
XLA Ops:
  6.5 1.6 slice.156
  8.2 4.5 collective-permute-start
  13.3 1.7 fusion.83
  15.0 1.3 compare_select_fusion.1
  17.2 6.2 %concatenate.3 = bf16[2,32,3,9792]{3,1,2,0:T(8,128)(2,1)} concatenate(bf16[2,32,3,4608]{3,1,2,0:T(8,128)(2,1)S(1)} %copy-done.13, bf16[2,32,3,3904]{3,1,2,0:T(8,128)(2,1)} %collective-permute-done, bf16[2,32,3,1280]{3,1,2,0:T(8,128)(2,1)S(1)} %broadcast_in_dim.2), dimensions={3} | concatenate | bytes 7520256 | tf_op jit(solution)/shard_map/concatenate | solution.py:25
  23.5 9.5 %fusion.82 = (bf16[2,32,3,9216]{3,1,2,0:T(8,128)(2,1)}, bf16[2,32,3,9216]{3,1,2,0:T(8,128)(2,1)S(1)}, bf16[2,32,3,9216]{3,1,2,0:T(8,128)(2,1)}, bf16[2,32,3,9216]{3,1,2,0:T(8,128)(2,1)}) fusion(bf16[2,32,3,9792]{3,1,2,0:T(8,128)(2,1)} %concatenate.3), kind=kLoop, calls=%fused_computation.133 | loop fusion | bytes 28311552 | tf_op jit(solution)/shard_map/slice | solution.py:31
  33.0 10.5 %stack_reshape.12 = bf16[2,32,3,12,3,1,256]{6,4,3,1,2,0,5:T(4,128)(2,1)} reshape(bf16[2,32,3,9216]{3,1,2,0:T(8,128)(2,1)} %get-tuple-element.26) | data formatting | bytes 7077888 | tf_op jit(solution)/shard_map/stack;reshape | solution.py:33
  43.5 6.2 %copy_dynamic-update-slice_fusion.3 = bf16[2,32,3,12,3,4,256]{6,1,5,4,3,2,0:T(8,128)(2,1)} fusion(bf16[2,32,3,12,3,1,256]{6,4,3,1,2,0,5:T(4,128)(2,1)} %stack_reshape.12), kind=kLoop, calls=%fused_computation.54 | loop fusion | bytes 7077888
  49.7 10.5 %stack_reshape.13 = bf16[2,32,3,12,3,1,256]{6,4,3,1,2,0,5:T(4,128)(2,1)} reshape(bf16[2,32,3,9216]{3,1,2,0:T(8,128)(2,1)} %get-tuple-element.25) | data formatting | bytes 7077888 | tf_op jit(solution)/shard_map/stack;reshape | solution.py:33
  60.2 7.5 %stack_reshape.14 = bf16[2,32,3,12,3,1,256]{6,4,3,1,2,0,5:T(4,128)(2,1)} reshape(bf16[2,32,3,9216]{3,1,2,0:T(8,128)(2,1)S(1)} %get-tuple-element.24) | data formatting | bytes 7077888 | tf_op jit(solution)/shard_map/stack;reshape | solution.py:33
  67.8 10.6 %stack_reshape.15 = bf16[2,32,3,12,3,1,256]{6,4,3,1,2,0,5:T(4,128)(2,1)} reshape(bf16[2,32,3,9216]{3,1,2,0:T(8,128)(2,1)} %get-tuple-element.23) | data formatting | bytes 7077888 | tf_op jit(solution)/shard_map/stack;reshape | solution.py:33
  78.4 6.4 %copy_dynamic-update-slice_fusion.2 = bf16[2,32,3,12,3,4,256]{6,1,5,4,3,2,0:T(8,128)(2,1)} fusion(bf16[2,32,3,12,3,4,256]{6,1,5,4,3,2,0:T(8,128)(2,1)} %copy_dynamic-update-slice_fusion.3, bf16[2,32,3,12,3,1,256]{6,4,3,1,2,0,5:T(4,128)(2,1)} %stack_reshape.13), kind=kLoop, calls=%fused_computation.53 | loop fusion | bytes 8257536
  84.8 3.8 copy_dynamic-update-slice_fusion.1
  88.6 3.8 copy_dynamic-update-slice_fusion
  92.4 27.3 %fusion.81 = (bf16[2,32,3,6,1,4,256]{6,1,5,4,3,2,0:T(8,128)(2,1)}, bf16[2,32,3,6,1,4,256]{6,1,5,4,3,2,0:T(8,128)(2,1)S(1)}, bf16[2,32,3,6,1,4,256]{6,1,5,4,3,2,0...) fusion(bf16[2,32,3,12,3,4,256]{6,1,5,4,3,2,0:T(8,128)(2,1)} %co, ...), kind=kLoop, calls=%fused_computation.132 | loop fusion | bytes 75497472 | tf_op jit(solution)/shard_map/slice | solution.py:39
  119.8 4.5 convert.35
  124.4 2.7 convert.36
  127.1 2.8 convert.37
  129.9 2.7 convert.38
  132.6 2.7 convert.39
  135.3 2.7 convert.40
  138.1 2.7 convert.41
  140.7 2.8 convert.42
  143.5 2.7 convert.43
  146.2 2.8 convert.44
  149.0 2.7 convert.45
  151.7 2.7 convert.46
  154.4 2.7 convert.47
  157.1 2.7 convert.48
  159.8 2.7 convert.49
  162.7 2.7 convert.50
  165.5 76.7 %fusion.10 = bf16[2,32,3,24,256]{4,3,2,1,0:T(8,128)(2,1)S(1)} fusion(f32[2,32,3,24,256]{4,1,3,2,0:T(8,128)} %convert.50, f32[2,32,3,24,256]{4,1,3,2,0:T(8,128)} %convert.49, f32[2,32,3,24,256]{4,1,3,2,0:T(8,128)} %convert.48, f32[2,32,3,24,256]{4,1,3,2,0:T(8,128)} %convert.47, f32[2,32,3,24,256]{4,1,3,2,0:T(8,128)} %convert.46, ...), kind=kLoop, calls=%fused_computation.21 | loop fusion | flops 37748736 | bytes 77873152 | tf_op jit(solution)/shard_map/convert_element_type | solution.py:44
  242.2 1.4 fusion.26
  243.6 1.4 fusion.25
  245.0 1.5 convolution_subtract_fusion
  246.5 1.9 subtract_convert_fusion.1
  248.5 4.5 copy.103
  253.0 4.5 copy.102
  257.5 52.5 %fusion.4 = f32[3,256,24,128]{3,2,1,0:T(8,128)S(1)} fusion(bf16[32,3,24,256]{0,2,3,1:T(8,128)(2,1)} %copy.103, f32[128,32]{0,1:T(8,128)S(1)} %get-tuple-element.46, s32[3,256]{1,0:T(4,128)S(1)} %copy-done.18, s32[128,32]{0,1:T(8,128)S(1)} %copy-done.35), kind=kOutput, calls=%fused_computation.14 | convolution fusion | flops 201326592 | bytes 10652672 | tf_op jit(solution)/shard_map/bsck,scfk->bcfk/dot_general | solution.py:97
  310.0 49.2 %fusion.3 = f32[3,256,24,128]{3,2,1,0:T(8,128)S(1)} fusion(bf16[32,3,24,256]{0,2,3,1:T(8,128)(2,1)S(1)} %copy-done.14, f32[128,32]{0,1:T(8,128)S(1)} %get-tuple-element.46, s32[3,256]{1,0:T(4,128)S(1)} %copy-done.18, s32[128,32]{0,1:T(8,128)S(1)} %copy-done.35), kind=kOutput, calls=%fused_computation.13 | convolution fusion | flops 201326592 | bytes 10652672 | tf_op jit(solution)/shard_map/bsck,scfk->bcfk/dot_general | solution.py:100
  359.2 55.3 %fusion.7 = bf16[128,1,3,24,256]{0,3,4,2,1:T(8,128)(2,1)} fusion(f32[3,256,24,128]{3,2,1,0:T(8,128)S(1)} %fusion.4, bf16[32,3,24,256]{0,2,3,1:T(8,128)(2,1)S(1)} %copy-done.14, s32[3,256]{1,0:T(4,128)S(1)} %copy-done.18, s32[128,32]{0,1:T(8,128)S(1)} %copy-done.35, f32[128,32]{0,1:T(8,128)S(1)} %copy-done.17), kind=kOutput, calls=%fused_computation.17 | convolution fusion | flops 206045184 | bytes 15371264 | tf_op jit(solution)/shard_map/bsck,scfk->bcfk/dot_general | solution.py:95
  414.5 55.3 %fusion.8 = bf16[128,1,3,24,256]{0,3,4,2,1:T(8,128)(2,1)} fusion(f32[3,256,24,128]{3,2,1,0:T(8,128)S(1)} %fusion.3, bf16[32,3,24,256]{0,2,3,1:T(8,128)(2,1)S(1)} %bitcast.136, s32[3,256]{1,0:T(4,128)S(1)} %copy-done.18, s32[128,32]{0,1:T(8,128)S(1)} %copy-done.35, f32[128,32]{0,1:T(8,128)S(1)} %copy-done.17), kind=kOutput, calls=%fused_computation.18 | convolution fusion | flops 206045184 | bytes 15371264 | tf_op jit(solution)/shard_map/bsck,scfk->bcfk/dot_general | solution.py:98
  469.8 8.3 %pad_maximum_fusion = bf16[128,2,3,24,256]{0,3,4,2,1:T(8,128)(2,1)} fusion(bf16[128,1,3,24,256]{0,3,4,2,1:T(8,128)(2,1)} %fusion.8, bf16[128,1,3,24,256]{0,3,4,2,1:T(8,128)(2,1)} %fusion.7), kind=kLoop, calls=%fused_computation.10 | loop fusion | flops 4718592 | bytes 18874368 | tf_op jit(solution)/shard_map/stack | solution.py:101
  478.1 13.9 %copy.106 = bf16[128,2,3,24,256]{4,3,2,1,0:T(8,128)(2,1)} copy(bf16[128,2,3,24,256]{0,3,4,2,1:T(8,128)(2,1)} %pad_maximum_fusion) | data formatting | bytes 18874368 | tf_op jit(solution)/shard_map/stack | solution.py:101
  492.0 88.3 %reduce-scatter.2.cloned.1.call-done = bf16[8,2,3,24,256]{4,3,2,1,0:T(8,128)(2,1)} async-done(((bf16[128,2,3,24,256]{4,3,2,1,0:T(8,128)(2,1)}), bf16[8,2,3,24,256]{4,3,2,1,0:T(8,128)(2,1)}) %reduce-scatter.2.cloned.1.call-update) | async-done | bytes 589840 | tf_op jit(solution)/shard_map/reduce_scatter | solution.py:123
  580.3 12.3 %all_to_all.27 = bf16[8,2,3,24,256]{4,3,2,1,0:T(8,128)(2,1)S(1)} all-to-all(bf16[8,2,3,24,256]{4,3,2,1,0:T(8,128)(2,1)} %reduce-scatter.2.cloned.1.call-done), channel_id=1, replica_groups=mesh['stn'=16,'chan'=4,'beam'=2] {'chan'}, dimensions={0} | all-to-all | bytes 1179648 | tf_op jit(solution)/shard_map/all_to_all | solution.py:130
  592.6 6.8 %all_to_all.28 = bf16[2,2,12,24,256]{4,3,2,1,0:T(8,128)(2,1)S(1)} all-to-all(bf16[2,2,12,24,256]{4,3,2,1,0:T(8,128)(2,1)S(1)} %bitcast.138), channel_id=1, replica_groups=mesh['stn'=16,'chan'=4,'beam'=2] {'beam'}, dimensions={0} | all-to-all | bytes 1179648 | tf_op jit(solution)/shard_map/all_to_all | solution.py:129
  599.5 1.2 copy.108
  (98 shorter events, 1.8 us)
Async XLA Ops:
  6.5 10.7 %copy-start.13 = (bf16[2,32,3,4608]{3,1,2,0:T(8,128)(2,1)S(1)}, bf16[2,32,3,4608]{3,1,2,0:T(8,128)(2,1)}, u32[]{:S(2)}) copy-start(bf16[2,32,3,4608]{3,1,2,0:T(8,128)(2,1)} %param.5) | copy-start | bytes 5308420
  6.5 573.8 %reduce-scatter.2.cloned.1.call-start = ((), (), s32[]{:S(2)}) async-start(), calls=%async_computation.3 | async-start | bytes 10027008 | tf_op jit(solution)/shard_map/reduce_scatter | solution.py:123
  8.2 9.0 %collective-permute-start = (bf16[2,32,3,3904]{3,1,2,0:T(8,128)(2,1)S(1)}, bf16[2,32,3,3904]{3,1,2,0:T(8,128)(2,1)}, u32[]{:S(2)}, u32[]{:S(2)}) collective-permute-start(bf16[2,32,3,3904]{3,1,2,0:T(8,128)(2,1)S(1)} %slice.156), channel_id=1, source_target_pairs={{1,0},{3,2},{5,4},{7,6},{9,8},{11,10},{13,12},{15,14},{17,16},{19,... | collective-permute-start | bytes 4497416 | tf_op jit(solution)/shard_map/ppermute | solution.py:14
  67.8 17.0 %slice-start = ((s8[4718592]{0:T(1024)(128)(4,1)}), s8[524288]{0:T(1024)(128)(4,1)S(1)}, s32[]{:S(2)}) async-start(s8[4718592]{0:T(1024)(128)(4,1)} %bitcast.115), calls=%async_computation.4 | async-start | bytes 1048576
  78.4 6.4 %slice-start.1 = ((s8[4718592]{0:T(1024)(128)(4,1)}), s8[4194304]{0:T(1024)(128)(4,1)S(1)}, s32[]{:S(2)}) async-start(s8[4718592]{0:T(1024)(128)(4,1)} %bitcast.115), calls=%async_computation.5 | async-start | bytes 8388608
  78.4 10.2 %slice-start.2 = ((s8[4718592]{0:T(1024)(128)(4,1)}), s8[4194304]{0:T(1024)(128)(4,1)S(1)}, s32[]{:S(2)}) async-start(s8[4718592]{0:T(1024)(128)(4,1)} %bitcast.117), calls=%async_computation.6 | async-start | bytes 8388608
  84.8 3.9 slice-start.3
  119.8 4.6 copy-start.12
  124.4 2.8 copy-start.11
  127.1 2.8 copy-start.10
  129.9 2.7 copy-start.9
  132.6 2.7 copy-start.8
  135.3 2.7 copy-start.7
  138.0 2.7 copy-start.6
  140.7 2.8 copy-start.5
  143.5 2.7 copy-start.4
  146.2 2.8 copy-start.3
  149.0 2.7 copy-start.2
  151.7 2.7 copy-start.1
  154.4 2.7 copy-start
  162.5 2.8 copy-start.19
  162.5 2.8 copy-start.20
  162.5 2.8 copy-start.21
  162.5 2.8 copy-start.22
  162.5 2.8 copy-start.23
  162.6 2.8 copy-start.24
  162.6 2.8 copy-start.25
  162.6 2.8 copy-start.26
  162.6 2.8 copy-start.27
  162.6 2.8 copy-start.28
  162.6 2.8 copy-start.29
  162.6 2.8 copy-start.30
  162.6 2.8 copy-start.31
  162.6 2.8 copy-start.32
  162.6 2.8 copy-start.33
  162.7 2.8 copy-start.34
  243.6 2.9 copy-start.15
  243.6 2.9 copy-start.16
  248.5 9.0 %copy-start.18 = (s32[3,256]{1,0:T(4,128)S(1)}, s32[3,256]{1,0:T(4,128)}, u32[]{:S(2)}) copy-start(s32[3,256]{1,0:T(4,128)} %iota_add_fusion) | copy-start | bytes 9220
  248.5 9.0 %copy-start.35 = (s32[128,32]{0,1:T(8,128)S(1)}, s32[128,32]{0,1:T(8,128)}, u32[]{:S(2)}) copy-start(s32[128,32]{0,1:T(8,128)} %param.7) | copy-start | bytes 49156
  257.5 52.5 %copy-start.14 = (bf16[32,3,24,256]{0,2,3,1:T(8,128)(2,1)S(1)}, bf16[32,3,24,256]{0,2,3,1:T(8,128)(2,1)}, u32[]{:S(2)}) copy-start(bf16[32,3,24,256]{0,2,3,1:T(8,128)(2,1)} %copy.102) | copy-start | bytes 3538948
  309.9 49.3 %copy-start.17 = (f32[128,32]{0,1:T(8,128)S(1)}, f32[128,32]{0,1:T(8,128)}, u32[]{:S(2)}) copy-start(f32[128,32]{0,1:T(8,128)} %get-tuple-element.45) | copy-start | bytes 49156
  310.0 104.6 %slice-start.4 = ((s8[4718592]{0:T(1024)(128)(4,1)}), s8[4194304]{0:T(1024)(128)(4,1)S(1)}, s32[]{:S(2)}) async-start(s8[4718592]{0:T(1024)(128)(4,1)} %bitcast.135), calls=%async_computation.8 | async-start | bytes 8388608
  359.2 55.3 %slice-start.5 = ((s8[4718592]{0:T(1024)(128)(4,1)}), s8[524288]{0:T(1024)(128)(4,1)S(1)}, s32[]{:S(2)}) async-start(s8[4718592]{0:T(1024)(128)(4,1)} %bitcast.135), calls=%async_computation.9 | async-start | bytes 1048576
Sparse Core Ops, SparseCore 0:
  492.1 88.1 reduce-scatter.1
where the time goes:
time: 618 us; the launch traced here: 608 us
  matrix products  218 us (35%)
  other arithmetic  133 us (22%)
  local copies, waits for them, and re-layouts  130 us (21%)
  waiting for transfers between devices  88.3 us (14%)
  blocking collectives  19.1 us (3%)
  between operations  14.3 us (2%)
    reduce_scatter x1, waiting for transfers between devices, body(): lax.psum_scatter(complex_form(weight_re, weight_im, spectra).astype(jnp.b...  88.3 us
    convert_element_type x1, other arithmetic, filter_frames(): return total.reshape(shape[:-1] + (frame_count, fine)).astype(jnp.bfloat16)  76.7 us
    dot_general x1, matrix products, complex_form(): jnp.einsum(form, weight_re, pieces[0], preferred_element_type=jnp.float32)  55.3 us
    dot_general x1, matrix products, complex_form(): jnp.einsum(form, weight_re, pieces[1], preferred_element_type=jnp.float32)  55.3 us
    dot_general x1, matrix products, complex_form(): jnp.einsum(form, weight_im, pieces[1], preferred_element_type=jnp.float32)  52.5 us
    dot_general x1, matrix products, complex_form(): jnp.einsum(form, weight_im, pieces[0], preferred_element_type=jnp.float32)  49.2 us
    convert_element_type x16, other arithmetic, filter_frames(): lax.slice_in_dim(stacked, lead, lead + groups, 1, axis)[..., inner, :, :]  45.3 us
    another operation x5, local copies, waits for them, and re-layouts, filter_frames(): stacked = jnp.stack(streams, axis=-2)  43 us
  transfers between devices with their start and end apart: 2, of which 1 were waited for; matrix products, arithmetic and copies ran while one was open for 1% of the time, Pallas kernels for 0%

commit v1 on v0

v1 whole, which is shorter than its diff:
```python
import functools
import math

import jax
import jax.numpy as jnp
from jax import lax
from jax.experimental import pallas as pl
from jax.experimental.pallas import tpu as pltpu
from jax.sharding import PartitionSpec as P

SUBARRAYS = 4
F32 = jnp.float32
BF16 = jnp.bfloat16
LANES = 128
NT = (((1,), (1,)), ((), ()))
NN = (((1,), (0,)), ((), ()))
START = (0, 0, 1, 2)
OFFSET = (0, 192, 128, 64)


def filter_tables(taps):
    count, fine = taps.shape
    lane = jnp.arange(fine, dtype=jnp.int32)
    tables = []
    for offset in OFFSET:
        rolled = jnp.roll(taps, offset, axis=1)
        early = jnp.pad(rolled, ((0, 1), (0, 0)))
        late = jnp.pad(rolled, ((1, 0), (0, 0)))
        tables.append(jnp.where(lane[None, :] >= offset, early, late))
    joined = jnp.concatenate(tables)
    return jnp.broadcast_to(joined[:, None, :], (joined.shape[0], 8, fine))


def dft_table(fine):
    index = jnp.arange(fine, dtype=jnp.int32)
    product = index[:, None] * index[None, :] % fine
    angle = 2.0 * jnp.pi * product.astype(F32) / fine
    scale = 1.0 / math.sqrt(fine)
    return jnp.concatenate(
        [(jnp.cos(angle) * scale).astype(BF16), (jnp.sin(angle) * scale).astype(BF16)], axis=1
    )


def tap_range(phase, tile, count):
    low, high = tile * LANES, (tile + 1) * LANES
    first = 1 if high <= OFFSET[phase] else 0
    last = count - 1 if low >= OFFSET[phase] else count
    return first, last


def channelize_kernel(count, core_ref, own_ref, other_ref, taps_ref, dft_ref, out_ref, x_ref, z_ref):
    half = own_ref.shape[-1]
    fine = taps_ref.shape[-1]
    blocks = 2 * half // fine
    groups = blocks // 3
    core = core_ref[0]
    own_at = pl.multiple_of(core * half, LANES)
    other_at = pl.multiple_of((1 - core) * half, LANES)
    own_row = pl.multiple_of(core * 16, 16)
    for part in range(2):
        x_ref[part, :, pl.ds(own_at, half)] = own_ref[part, 0, pl.ds(own_row, 16), :]
        x_ref[part, :, pl.ds(other_at, half)] = other_ref[part, 0]
    frames = 4 * groups
    rows = 2 * frames
    tiles = fine // LANES
    for tile in range(tiles):
        for group in range(groups):
            sums = [[[None, None] for _ in range(2)] for _ in range(4)]
            for step in range(count + 3):
                block = 3 * group + step
                if block >= blocks:
                    break
                uses = []
                for phase in range(4):
                    first, last = tap_range(phase, tile, count)
                    tap = step - START[phase]
                    if first <= tap <= last:
                        uses.append((phase, tap))
                if not uses:
                    continue
                at = block * fine + tile * LANES
                data = [x_ref[part, :, pl.ds(at, LANES)].astype(F32) for part in range(2)]
                for phase, tap in uses:
                    weight = taps_ref[phase * (count + 1) + tap, :, pl.ds(tile * LANES, LANES)]
                    for part in range(2):
                        for side in range(2):
                            term = weight * data[part][8 * side : 8 * side + 8]
                            old = sums[phase][part][side]
                            sums[phase][part][side] = term if old is None else old + term
            for phase in range(4):
                frame = 4 * group + phase
                for side in range(2):
                    real, imag = sums[phase][0][side], sums[phase][1][side]
                    base = side * 8 * rows + frame
                    top = pl.ds(base, 8, stride=rows)
                    low = pl.ds(base + frames, 8, stride=rows)
                    z_ref[tile, top, :] = real
                    z_ref[tiles + tile, top, :] = imag
                    z_ref[tile, low, :] = imag
                    z_ref[tiles + tile, low, :] = -real
    table = dft_ref[...]
    piece = rows // 3
    dests = out_ref.shape[0]
    for pair in range(2):
        results = []
        for quad in (2 * pair, 2 * pair + 1):
            order = []
            for member in range(3):
                start = (4 * quad + member) * rows
                order.append((start, rows))
                order.append(((4 * quad + 3) * rows + member * piece, piece))
            operand = jnp.concatenate(
                [
                    jnp.concatenate(
                        [z_ref[lane, pl.ds(start, size), :] for lane in range(2 * tiles)], axis=1
                    ).astype(BF16)
                    for start, size in order
                ],
                axis=0,
            )
            found = lax.dot_general(table, operand, NT, preferred_element_type=F32)
            results.append(found.reshape(dests, fine // dests, 4 * rows))
        out_ref[:, 0, pl.ds(16 * pair, 16), :] = jnp.concatenate(results, axis=1).astype(BF16)


def turn_parts(turn):
    quadrant = lax.shift_right_logical(turn + 8192, 14)
    x = (turn - quadrant * 16384).astype(F32) * (2.0 * math.pi / 65536.0)
    y = x * x
    sine = x * (1.0 + y * (-1.0 / 6 + y * (1.0 / 120 + y * (-1.0 / 5040 + y * (1.0 / 362880)))))
    cosine = 1.0 + y * (-0.5 + y * (1.0 / 24 + y * (-1.0 / 720 + y * (1.0 / 40320))))
    odd = (quadrant & 1) == 1
    cos_part = jnp.where(odd, sine, cosine)
    sin_part = jnp.where(odd, cosine, sine)
    cos_part = jnp.where(((quadrant + 1) & 2) == 2, -cos_part, cos_part)
    sin_part = jnp.where((quadrant & 2) == 2, -sin_part, sin_part)
    return cos_part, sin_part


def beam_kernel(
    amplitude, fine, place_ref, code_ref, data_ref, out_ref, delay_ref, flat_ref, weight_ref, sum_ref
):
    coarse = pl.program_id(0)
    sources = data_ref.shape[0]
    beams = out_ref.shape[0]
    near = out_ref.shape[2]
    quads = data_ref.shape[2] // near
    depth = sources * quads
    stations = 4 * depth

    @pl.when(coarse == 0)
    def _():
        for member in range(4):
            for index in range(code_ref.shape[0]):
                width = code_ref.shape[2]
                delay_ref[pl.ds(member * depth + index * width, width), :] = code_ref[index, member]

    freq = (place_ref[0] + coarse) * fine + place_ref[1]
    strip = 32
    for member in range(4):
        lanes = pl.ds(member * depth, depth)
        turned = jnp.transpose(delay_ref[lanes, :].astype(F32)).astype(jnp.int32)
        for top in range(0, beams, strip):
            delay = turned[top : top + strip]
            scale = jnp.where(delay >= 0, amplitude, 0.0).astype(F32)
            delay = jnp.maximum(delay, 0)
            cos_part, sin_part = turn_parts((delay * freq) & 65535)
            cos_step, sin_step = turn_parts(delay)
            real, imag = cos_part * scale, -(sin_part * scale)
            for step in range(near):
                weight_ref[step, pl.ds(top, strip), lanes] = real.astype(BF16)
                weight_ref[step, pl.ds(beams + top, strip), lanes] = imag.astype(BF16)
                if step + 1 < near:
                    real, imag = (
                        real * cos_step + imag * sin_step,
                        imag * cos_step - real * sin_step,
                    )

    for tile in range(3):
        flat_ref[tile] = (
            data_ref[:, 0, :, pl.ds(tile * LANES, LANES)]
            .astype(F32)
            .reshape(sources * quads * near, LANES)
        )
    lane = lax.broadcasted_iota(jnp.int32, (depth, LANES), 1)
    lane_out = lax.broadcasted_iota(jnp.int32, (beams, LANES), 1)
    for step in range(near):
        pieces = [flat_ref[tile, pl.ds(step, depth, stride=near), :] for tile in range(3)]
        last = jnp.where(
            lane < 32,
            pltpu.roll(pieces[0], 32, 1),
            jnp.where(lane < 64, pltpu.roll(pieces[1], 64, 1), pltpu.roll(pieces[2], 96, 1)),
        )
        operand = jnp.concatenate([piece.astype(BF16) for piece in pieces + [last]], axis=0)
        found = lax.dot_general(weight_ref[step], operand, NN, preferred_element_type=F32)
        by_real, by_imag = found[:beams], found[beams:]
        crossed = jnp.where(lane_out < 48, -pltpu.roll(by_imag, 80, 1), pltpu.roll(by_imag, 48, 1))
        sum_ref[pl.ds(step, beams, stride=near), :] = by_real + crossed
    out_ref[:, 0] = sum_ref[...].reshape(beams, near, LANES).astype(BF16)


def order_kernel(data_ref, out_ref):
    coarse, frames, fine = out_ref.shape[2:]
    width = 2 * frames
    row = lax.broadcasted_iota(jnp.int32, (width, LANES), 0)
    column = lax.broadcasted_iota(jnp.int32, (width, LANES), 1)
    unit = (row == column).astype(F32).astype(BF16)
    keep = lax.broadcasted_iota(jnp.int32, (fine, LANES), 1) < width
    for index in range(coarse):
        block = data_ref[:, 0, :, index].astype(F32).reshape(fine, LANES)
        block = jnp.where(keep, block, 0.0).astype(BF16)
        found = lax.dot_general(unit, block, NT, preferred_element_type=F32)
        out_ref[0, 0, index] = found[:frames]
        out_ref[0, 1, index] = found[frames:]


def body(volts, taps, delays, station_sub, beam_sub):
    count, fine = taps.shape
    stations, coarse, half = volts.shape[1:]
    beams = beam_sub.shape[0]
    stn, chan, beam = (lax.axis_size(name) for name in ("stn", "chan", "beam"))
    core = lax.axis_index("beam")
    dests = stn * beam
    near = fine // dests
    frames = beam * half // (3 * fine // 4)
    own = stations // beam
    amplitude = 1.0 / math.sqrt(stations * stn // SUBARRAYS)

    arranged = jnp.transpose(volts, (0, 2, 1, 3))
    away = lax.dynamic_slice_in_dim(arranged, (1 - core) * own, own, 2)
    other = lax.ppermute(away, "beam", [(0, 1), (1, 0)])

    code = jnp.where(station_sub[:, None] == beam_sub[None, :], delays.T, -1)
    code = code.reshape(stations // 4, 4, beams).transpose(1, 0, 2)
    codes = lax.all_gather(code, "stn")

    spectra = pl.pallas_call(
        functools.partial(channelize_kernel, count),
        grid=(coarse,),
        out_shape=jax.ShapeDtypeStruct((dests, coarse, own // 4 * near, 8 * frames), BF16),
        in_specs=[
            pl.BlockSpec(memory_space=pltpu.SMEM),
            pl.BlockSpec((2, 1, stations, half), lambda c: (0, c, 0, 0)),
            pl.BlockSpec((2, 1, own, half), lambda c: (0, c, 0, 0)),
            pl.BlockSpec((4 * (count + 1), 8, fine), lambda c: (0, 0, 0)),
            pl.BlockSpec((fine, 2 * fine), lambda c: (0, 0)),
        ],
        out_specs=pl.BlockSpec((dests, 1, own // 4 * near, 8 * frames), lambda c: (0, c, 0, 0)),
        scratch_shapes=[
            pltpu.VMEM((2, own, beam * half), BF16),
            pltpu.VMEM((2 * fine // LANES, own * 2 * frames, LANES), F32),
        ],
        compiler_params=pltpu.CompilerParams(vmem_limit_bytes=40 * 2**20),
        name="channelize",
    )(core.reshape(1), arranged, other, filter_tables(taps), dft_table(fine))

    mixed = lax.all_to_all(spectra, ("stn", "beam"), 0, 0, tiled=True)

    place = jnp.stack(
        [lax.axis_index("chan") * coarse, (lax.axis_index("stn") * beam + core) * near]
    ).astype(jnp.int32)
    total = stations * stn
    formed = pl.pallas_call(
        functools.partial(beam_kernel, amplitude, fine),
        grid=(coarse,),
        out_shape=jax.ShapeDtypeStruct((beams, coarse, near, LANES), BF16),
        in_specs=[
            pl.BlockSpec(memory_space=pltpu.SMEM),
            pl.BlockSpec((stn, 4, stations // 4, beams), lambda c: (0, 0, 0, 0)),
            pl.BlockSpec((dests, 1, own // 4 * near, 8 * frames), lambda c: (0, c, 0, 0)),
        ],
        out_specs=pl.BlockSpec((beams, 1, near, LANES), lambda c: (0, c, 0, 0)),
        scratch_shapes=[
            pltpu.VMEM((total, beams), jnp.int32),
            pltpu.VMEM((3, total // 4 * near, LANES), F32),
            pltpu.VMEM((near, 2 * beams, total), BF16),
            pltpu.VMEM((beams * near, LANES), F32),
        ],
        compiler_params=pltpu.CompilerParams(vmem_limit_bytes=40 * 2**20),
        name="beamform",
    )(place, codes, mixed)

    owned = lax.all_to_all(formed, ("stn", "chan", "beam"), 0, 0, tiled=True)
    owned = owned.reshape(stn, chan, beam, coarse, near, LANES)
    return pl.pallas_call(
        order_kernel,
        grid=(chan,),
        out_shape=jax.ShapeDtypeStruct((1, 2, chan * coarse, frames, fine), F32),
        in_specs=[
            pl.BlockSpec((stn, 1, beam, coarse, near, LANES), lambda z: (0, z, 0, 0, 0, 0))
        ],
        out_specs=pl.BlockSpec((1, 2, coarse, frames, fine), lambda z: (0, 0, z, 0, 0)),
        compiler_params=pltpu.CompilerParams(vmem_limit_bytes=32 * 2**20),
        name="order",
    )(owned)


def solution(mesh):
    placed = (P(None, "stn", "chan", "beam"), P(), P(None, "stn"), P("stn"), P())
    return jax.shard_map(
        body,
        mesh=mesh,
        in_specs=placed,
        out_specs=P(("stn", "chan", "beam"), None, None, None, None),
        check_vma=False,
    )
```

time: 618 us -> 108 us (0.17); the launches traced: 608 us -> 108 us
  matrix products: 218 us -> 0 us
  other arithmetic: 133 us -> 1.41 us
  local copies, waits for them, and re-layouts: 130 us -> 2.98 us
  waiting for transfers between devices: 88.3 us -> 0.57 us
  blocking collectives: 19.1 us -> 70.8 us
  Pallas kernels: 0 us -> 22.4 us
  between operations: 14.3 us -> 0.16 us
    dot_general x8 -> x0, matrix products: 218 us -> none  [the longest x1 55.3 us: complex_form(): jnp.einsum(form, weight_re, pieces[0], preferred_element_type=jnp.float32)]
    convert_element_type x18 -> x1, other arithmetic: 122 us -> 1.11 us  [dft_table(): (jnp.sin(angle) * scale).astype(BF16)]
    reduce_scatter x1 -> x0, waiting for transfers between devices: 88.3 us -> none  [body(): lax.psum_scatter(complex_form(weight_re, weight_im, spectra).astype(jnp.b...]
    another operation x6 -> x0, local copies, waits for them, and re-layouts: 56.9 us -> none  [the longest x5 43 us: filter_frames(): stacked = jnp.stack(streams, axis=-2)]
    all_gather x0 -> x1, blocking collectives: none -> 41.4 us  [body(): codes = lax.all_gather(code, 'stn')]
    slice x4 -> x3, local copies, waits for them, and re-layouts: 40.2 us -> 0.15 us  [filter_tables(): rolled = jnp.roll(taps, offset, axis=1)]
    pallas_call x0 -> x3, Pallas kernels: none -> 22.4 us  [the longest x1 12.2 us: body(): pl.pallas_call(functools.partial(channelize_kernel, count), grid=(coarse,...]
    unnamed x87 -> x12, local copies, waits for them, and re-layouts: 16.6 us -> 1.43 us
where the time goes in v1:
time: 108 us
  blocking collectives  70.8 us (66%)
  Pallas kernels  22.4 us (21%)
  starting transfers between devices  9.17 us (8%)
  local copies, waits for them, and re-layouts  2.98 us (3%)
  other arithmetic  1.41 us (1%)
    all_gather x1, blocking collectives, body(): codes = lax.all_gather(code, 'stn')  41.4 us
    all_to_all x1, blocking collectives, body(): owned = lax.all_to_all(formed, ('stn', 'chan', 'beam'), 0, 0, tiled=True)  29.5 us
    pallas_call x1, Pallas kernels, body(): pl.pallas_call(functools.partial(channelize_kernel, count), grid=(coarse,...  12.2 us
    pallas_call x1, Pallas kernels, body(): pl.pallas_call(functools.partial(beam_kernel, amplitude, fine), grid=(coa...  8.09 us
    all_to_all x1, starting transfers between devices, body(): mixed = lax.all_to_all(spectra, ('stn', 'beam'), 0, 0, tiled=True)  7.67 us
  transfers between devices with their start and end apart: 2, of which 1 were waited for; matrix products, arithmetic and copies ran while one was open for 1% of the time, Pallas kernels for 0%

profile of v1, /device:TPU:1, one launch (start us, length us, event | category | flops | bytes accessed | tf_op | source)
XLA Modules:
  0.0 107.5 jit_solution(13645234476355562981)
XLA Ops:
  0.0 0.0 copy-start.2
  0.0 0.0 copy-start.1
  0.0 1.4 %dynamic-slice_bitcast_fusion = bf16[2,3,16,4608]{3,2,1,0:T(8,128)(2,1)S(1)} fusion(bf16[2,32,3,4608]{3,1,2,0:T(8,128)(2,1)} %param.5, s32[]{:T(128)S(6)} %select_n.28), kind=kLoop, calls=%fused_computation | loop fusion | bytes 1769476 | tf_op jit(solution)/shard_map/dynamic_slice | solution.py:230
  1.4 1.5 %collective-permute-start = (bf16[2,3,16,4608]{3,2,1,0:T(8,128)(2,1)S(1)}, bf16[2,3,16,4608]{3,2,1,0:T(8,128)(2,1)S(1)}, u32[]{:S(2)}, u32[]{:S(2)}) collective-permute-start(bf16[2,3,16,4608]{3,2,1,0:T(8,128)(2,1)S(1)} %dynamic-slice_bitcast_fusion), channel_id=1, source_target_pairs={{0,1},{1,0},{2,3},{3,2},{4,5},{5,4},{6,7},{7,6},{8,9},{9,8},{10,11... | collective-permute-start | bytes 2654216 | tf_op jit(solution)/shard_map/ppermute | solution.py:231
  2.9 0.0 copy-done.2
  2.9 0.1 fusion.8
  2.9 0.1 fusion.9
  3.0 0.1 pad_maximum_fusion.1
  3.2 1.1 %multiply_convert_fusion = (bf16[256,256]{1,0:T(8,128)(2,1)S(1)}, bf16[256,256]{1,0:T(8,128)(2,1)S(1)}) fusion(), kind=kLoop, calls=%fused_computation.8 | loop fusion | flops 1179648 | bytes 262144 | tf_op jit(solution)/shard_map/convert_element_type | solution.py:40
  4.3 0.6 collective-permute-done.other_ref
  5.0 0.0 copy-done.1
  5.0 12.2 %channelize.1 = bf16[32,3,32,384]{3,2,1,0:T(8,128)(2,1)S(1)} custom-call(s32[1]{0:T(128)} %bitcast.6.core_ref, bf16[2,3,32,4608]{3,2,1,0:T(8,128)(2,1)S(1)} %bitcast.13, bf16[2,3,16,4608]{3,2,1,0:T(8,128)(2,1)S(1)} %collective-permute-done.other_ref, f32[68,8,256]{2,1,0:T(8,128)S(1)} %broadcast_in_dim.43.taps_ref, bf16[256,512]{1,0:T(8,128)(2,1)S(1)} %pad_maximum_fusion.dft_ref), custom_call_target="tpu_custom_call" | custom-call | tf_op jit(solution)/shard_map/channelize/pallas_call | solution.py:237
  17.2 0.0 copy-start
  17.2 1.4 %copy-done = bf16[32,3,32,384]{3,2,1,0:T(8,128)(2,1)} copy-done((bf16[32,3,32,384]{3,2,1,0:T(8,128)(2,1)}, bf16[32,3,32,384]{3,2,1,0:T(8,128)(2,1)S(1)}, u32[]{:S(2)}) %copy-start) | copy-done | bytes 2359320
  18.6 0.0 copy-start.3
  18.6 0.0 copy-start.4
  18.6 0.0 copy-start.5
  18.6 7.7 %all-to-all-start = ((bf16[32,3,32,384]{3,2,1,0:T(8,128)(2,1)}), bf16[32,3,32,384]{3,2,1,0:T(8,128)(2,1)S(1)}, u32[]{:S(2)}, u32[]{:S(2)}) async-start(bf16[32,3,32,384]{3,2,1,0:T(8,128)(2,1)} %copy-done), calls=%async_computation | async-start | bytes 4718592 | tf_op jit(solution)/shard_map/all_to_all | solution.py:257
  26.3 0.0 copy-done.3
  26.3 0.0 copy-done.4
  26.3 0.0 copy-done.5
  26.3 0.1 bitcast_select_fusion
  26.4 41.4 %all-gather = s32[64,8,128]{2,1,0:T(8,128)S(1)} all-gather(s32[4,8,128]{2,1,0:T(8,128)S(1)} %copy.7), channel_id=2, replica_groups=mesh['stn'=16,'chan'=4,'beam'=2] {'stn'}, dimensions={0}, use_global_device_ids=true | all-gather | bytes 278528 | tf_op jit(solution)/shard_map/all_gather | solution.py:235
  67.8 0.1 pad_add_fusion.place_ref
  67.9 0.0 all-to-all-done.data_ref
  67.9 8.1 %beamform.1 = bf16[128,3,8,128]{3,2,1,0:T(8,128)(2,1)S(1)} custom-call(s32[2]{0:T(128)S(1)} %pad_add_fusion.place_ref, s32[16,4,8,128]{3,2,1,0:T(8,128)S(1)} %bitcast.15, bf16[32,3,32,384]{3,2,1,0:T(8,128)(2,1)S(1)} %all-to-all-done.data_ref), custom_call_target="tpu_custom_call" | custom-call | tf_op jit(solution)/shard_map/beamform/pallas_call | solution.py:263
  76.0 29.5 %all_to_all.10 = bf16[128,3,8,128]{3,2,1,0:T(8,128)(2,1)S(1)} all-to-all(bf16[128,3,8,128]{3,2,1,0:T(8,128)(2,1)S(1)} %beamform.1), channel_id=1, replica_groups=mesh['stn'=16,'chan'=4,'beam'=2] {'stn','chan','beam'}, dimensions={0} | all-to-all | bytes 1572864 | tf_op jit(solution)/shard_map/all_to_all | solution.py:283
  105.4 2.1 %order.1 = f32[1,2,12,48,256]{4,3,2,1,0:T(8,128)} custom-call(bf16[16,4,2,3,8,128]{5,4,3,2,1,0:T(8,128)(2,1)S(1)} %bitcast.14), custom_call_target="tpu_custom_call" | custom-call | tf_op jit(solution)/shard_map/order/pallas_call | solution.py:285
  (12 shorter events, 0.1 us)
Async XLA Ops:
  0.0 2.9 %copy-start.2 = (f32[16,256]{1,0:T(8,128)S(1)}, f32[16,256]{1,0:T(8,128)}, u32[]{:S(2)}) copy-start(f32[16,256]{1,0:T(8,128)} %param.6) | copy-start | bytes 49156
  0.0 5.0 %copy-start.1 = (bf16[2,32,3,4608]{3,1,2,0:T(8,128)(2,1)S(1)}, bf16[2,32,3,4608]{3,1,2,0:T(8,128)(2,1)}, u32[]{:S(2)}) copy-start(bf16[2,32,3,4608]{3,1,2,0:T(8,128)(2,1)} %param.5) | copy-start | bytes 5308420
  1.4 3.6 %collective-permute-start = (bf16[2,3,16,4608]{3,2,1,0:T(8,128)(2,1)S(1)}, bf16[2,3,16,4608]{3,2,1,0:T(8,128)(2,1)S(1)}, u32[]{:S(2)}, u32[]{:S(2)}) collective-permute-start(bf16[2,3,16,4608]{3,2,1,0:T(8,128)(2,1)S(1)} %dynamic-slice_bitcast_fusion), channel_id=1, source_target_pairs={{0,1},{1,0},{2,3},{3,2},{4,5},{5,4},{6,7},{7,6},{8,9},{9,8},{10,11... | collective-permute-start | bytes 2654216 | tf_op jit(solution)/shard_map/ppermute | solution.py:231
  17.2 1.4 %copy-start = (bf16[32,3,32,384]{3,2,1,0:T(8,128)(2,1)}, bf16[32,3,32,384]{3,2,1,0:T(8,128)(2,1)S(1)}, u32[]{:S(2)}) copy-start(bf16[32,3,32,384]{3,2,1,0:T(8,128)(2,1)S(1)} %channelize.1) | copy-start | bytes 7077892
  18.6 7.7 %copy-start.3 = (s32[128,32]{0,1:T(8,128)S(1)}, s32[128,32]{0,1:T(8,128)}, u32[]{:S(2)}) copy-start(s32[128,32]{0,1:T(8,128)} %param.7) | copy-start | bytes 49156
  18.6 7.7 %copy-start.4 = (s32[128]{0:T(128)S(1)}, s32[128]{0:T(128)}, u32[]{:S(2)}) copy-start(s32[128]{0:T(128)} %param.9) | copy-start | bytes 1540
  18.6 7.7 %copy-start.5 = (s32[32]{0:T(128)S(1)}, s32[32]{0:T(128)}, u32[]{:S(2)}) copy-start(s32[32]{0:T(128)} %param.8) | copy-start | bytes 388
  18.6 49.2 %all-to-all-start = ((bf16[32,3,32,384]{3,2,1,0:T(8,128)(2,1)}), bf16[32,3,32,384]{3,2,1,0:T(8,128)(2,1)S(1)}, u32[]{:S(2)}, u32[]{:S(2)}) async-start(bf16[32,3,32,384]{3,2,1,0:T(8,128)(2,1)} %copy-done), calls=%async_computation | async-start | bytes 4718592 | tf_op jit(solution)/shard_map/all_to_all | solution.py:257

commit v2 on v1

--- a/solution.py
+++ b/solution.py
@@ -3,6 +3,8 @@
 
 import jax
 import jax.numpy as jnp
+import ml_dtypes
+import numpy as np
 from jax import lax
 from jax.experimental import pallas as pl
 from jax.experimental.pallas import tpu as pltpu
@@ -12,33 +14,32 @@
 F32 = jnp.float32
 BF16 = jnp.bfloat16
 LANES = 128
+PITCH = 9
 NT = (((1,), (1,)), ((), ()))
 NN = (((1,), (0,)), ((), ()))
 START = (0, 0, 1, 2)
 OFFSET = (0, 192, 128, 64)
 
 
-def filter_tables(taps):
-    count, fine = taps.shape
-    lane = jnp.arange(fine, dtype=jnp.int32)
-    tables = []
-    for offset in OFFSET:
-        rolled = jnp.roll(taps, offset, axis=1)
-        early = jnp.pad(rolled, ((0, 1), (0, 0)))
-        late = jnp.pad(rolled, ((1, 0), (0, 0)))
-        tables.append(jnp.where(lane[None, :] >= offset, early, late))
-    joined = jnp.concatenate(tables)
-    return jnp.broadcast_to(joined[:, None, :], (joined.shape[0], 8, fine))
+def fill_filter_tables(taps_ref, wide_ref):
+    count, fine = taps_ref.shape
+    taps = taps_ref[...]
+    lane = lax.broadcasted_iota(jnp.int32, (1, fine), 1)
+    for phase, offset in enumerate(OFFSET):
+        rolled = pltpu.roll(taps, offset, 1) if offset else taps
+        for tap in range(count + 1):
+            early, late = rolled[min(tap, count - 1)], rolled[max(tap - 1, 0)]
+            early = early[None] if tap < count else jnp.zeros((1, fine), F32)
+            late = late[None] if tap > 0 else jnp.zeros((1, fine), F32)
+            row = jnp.where(lane >= offset, early, late)
+            wide_ref[phase * (count + 1) + tap] = jnp.broadcast_to(row, (8, fine))
 
 
 def dft_table(fine):
-    index = jnp.arange(fine, dtype=jnp.int32)
-    product = index[:, None] * index[None, :] % fine
-    angle = 2.0 * jnp.pi * product.astype(F32) / fine
-    scale = 1.0 / math.sqrt(fine)
-    return jnp.concatenate(
-        [(jnp.cos(angle) * scale).astype(BF16), (jnp.sin(angle) * scale).astype(BF16)], axis=1
-    )
+    index = np.arange(fine)
+    angle = 2.0 * np.pi * (index[:, None] * index[None, :] % fine) / fine
+    table = np.concatenate([np.cos(angle), np.sin(angle)], axis=1) / math.sqrt(fine)
+    return jnp.asarray(table.astype(np.float32).astype(ml_dtypes.bfloat16))
 
 
 def tap_range(phase, tile, count):
@@ -48,7 +49,15 @@
     return first, last
 
 
-def channelize_kernel(count, core_ref, own_ref, other_ref, taps_ref, dft_ref, out_ref, x_ref, z_ref):
+def channelize_kernel(
+    core_ref, own_ref, other_ref, prototype_ref, dft_ref, out_ref, x_ref, z_ref, taps_ref
+):
+    count = prototype_ref.shape[0]
+
+    @pl.when(pl.program_id(0) == 0)
+    def _():
+        fill_filter_tables(prototype_ref, taps_ref)
+
     half = own_ref.shape[-1]
     fine = taps_ref.shape[-1]
     blocks = 2 * half // fine
@@ -62,6 +71,7 @@
         x_ref[part, :, pl.ds(other_at, half)] = other_ref[part, 0]
     frames = 4 * groups
     rows = 2 * frames
+    depth = PITCH * rows
     tiles = fine // LANES
     for tile in range(tiles):
         for group in range(groups):
@@ -91,9 +101,9 @@
                 frame = 4 * group + phase
                 for side in range(2):
                     real, imag = sums[phase][0][side], sums[phase][1][side]
-                    base = side * 8 * rows + frame
-                    top = pl.ds(base, 8, stride=rows)
-                    low = pl.ds(base + frames, 8, stride=rows)
+                    base = side * depth + PITCH * frame
+                    top = pl.ds(base, 8)
+                    low = pl.ds(base + PITCH * frames, 8)
                     z_ref[tile, top, :] = real
                     z_ref[tiles + tile, top, :] = imag
                     z_ref[tile, low, :] = imag
@@ -105,14 +115,14 @@
         results = []
         for quad in (2 * pair, 2 * pair + 1):
             order = []
+            base = pair * depth + 4 * (quad % 2)
             for member in range(3):
-                start = (4 * quad + member) * rows
-                order.append((start, rows))
-                order.append(((4 * quad + 3) * rows + member * piece, piece))
+                order.append((base + member, rows))
+                order.append((base + 3 + PITCH * member * piece, piece))
             operand = jnp.concatenate(
                 [
                     jnp.concatenate(
-                        [z_ref[lane, pl.ds(start, size), :] for lane in range(2 * tiles)], axis=1
+                        [z_ref[lane, pl.ds(start, size, stride=PITCH), :] for lane in range(2 * tiles)], axis=1
                     ).astype(BF16)
                     for start, size in order
                 ],
@@ -137,22 +147,17 @@
     return cos_part, sin_part
 
 
-def beam_kernel(
-    amplitude, fine, place_ref, code_ref, data_ref, out_ref, delay_ref, flat_ref, weight_ref, sum_ref
-):
+def weight_kernel(amplitude, fine, place_ref, code_ref, weight_ref, delay_ref):
+    near, rows, stations = weight_ref.shape[1:]
+    beams = rows // 2
+    depth = stations // 4
     coarse = pl.program_id(0)
-    sources = data_ref.shape[0]
-    beams = out_ref.shape[0]
-    near = out_ref.shape[2]
-    quads = data_ref.shape[2] // near
-    depth = sources * quads
-    stations = 4 * depth
 
     @pl.when(coarse == 0)
     def _():
-        for member in range(4):
-            for index in range(code_ref.shape[0]):
-                width = code_ref.shape[2]
+        width = code_ref.shape[2]
+        for index in range(code_ref.shape[0]):
+            for member in range(4):
                 delay_ref[pl.ds(member * depth + index * width, width), :] = code_ref[index, member]
 
     freq = (place_ref[0] + coarse) * fine + place_ref[1]
@@ -168,35 +173,43 @@
             cos_step, sin_step = turn_parts(delay)
             real, imag = cos_part * scale, -(sin_part * scale)
             for step in range(near):
-                weight_ref[step, pl.ds(top, strip), lanes] = real.astype(BF16)
-                weight_ref[step, pl.ds(beams + top, strip), lanes] = imag.astype(BF16)
+                weight_ref[0, step, pl.ds(top, strip), lanes] = real.astype(BF16)
+                weight_ref[0, step, pl.ds(beams + top, strip), lanes] = imag.astype(BF16)
                 if step + 1 < near:
                     real, imag = (
                         real * cos_step + imag * sin_step,
                         imag * cos_step - real * sin_step,
                     )
 
+
+def beam_kernel(weight_ref, data_ref, out_ref, flat_ref, sum_ref):
+    sources = data_ref.shape[0]
+    beams = out_ref.shape[0]
+    near = out_ref.shape[2]
+    quads = data_ref.shape[2] // near
+    depth = sources * quads
     for tile in range(3):
-        flat_ref[tile] = (
-            data_ref[:, 0, :, pl.ds(tile * LANES, LANES)]
-            .astype(F32)
-            .reshape(sources * quads * near, LANES)
-        )
+        for source in range(sources):
+            block = data_ref[source, 0, :, pl.ds(tile * LANES, LANES)].astype(F32)
+            for quad in range(quads):
+                row = PITCH * (source * quads + quad)
+                flat_ref[tile, pl.ds(row, near), :] = block[quad * near : (quad + 1) * near]
     lane = lax.broadcasted_iota(jnp.int32, (depth, LANES), 1)
     lane_out = lax.broadcasted_iota(jnp.int32, (beams, LANES), 1)
     for step in range(near):
-        pieces = [flat_ref[tile, pl.ds(step, depth, stride=near), :] for tile in range(3)]
+        pieces = [flat_ref[tile, pl.ds(step, depth, stride=PITCH), :] for tile in range(3)]
         last = jnp.where(
             lane < 32,
             pltpu.roll(pieces[0], 32, 1),
             jnp.where(lane < 64, pltpu.roll(pieces[1], 64, 1), pltpu.roll(pieces[2], 96, 1)),
         )
         operand = jnp.concatenate([piece.astype(BF16) for piece in pieces + [last]], axis=0)
-        found = lax.dot_general(weight_ref[step], operand, NN, preferred_element_type=F32)
+        found = lax.dot_general(weight_ref[0, step], operand, NN, preferred_element_type=F32)
         by_real, by_imag = found[:beams], found[beams:]
         crossed = jnp.where(lane_out < 48, -pltpu.roll(by_imag, 80, 1), pltpu.roll(by_imag, 48, 1))
-        sum_ref[pl.ds(step, beams, stride=near), :] = by_real + crossed
-    out_ref[:, 0] = sum_ref[...].reshape(beams, near, LANES).astype(BF16)
+        sum_ref[pl.ds(step, beams, stride=PITCH), :] = by_real + crossed
+    for index in range(beams):
+        out_ref[index, 0] = sum_ref[pl.ds(PITCH * index, near), :].astype(BF16)
 
 
 def order_kernel(data_ref, out_ref):
@@ -214,6 +227,10 @@
         out_ref[0, 1, index] = found[frames:]
 
 
+def in_hbm(array):
+    return pltpu.with_memory_space_constraint(array, pltpu.HBM)
+
+
 def body(volts, taps, delays, station_sub, beam_sub):
     count, fine = taps.shape
     stations, coarse, half = volts.shape[1:]
@@ -232,53 +249,69 @@
 
     code = jnp.where(station_sub[:, None] == beam_sub[None, :], delays.T, -1)
     code = code.reshape(stations // 4, 4, beams).transpose(1, 0, 2)
-    codes = lax.all_gather(code, "stn")
+    copies = jnp.broadcast_to(code, (stn,) + code.shape)
+    codes = lax.all_to_all(lax.optimization_barrier(copies), "stn", 0, 0, tiled=True)
 
     spectra = pl.pallas_call(
-        functools.partial(channelize_kernel, count),
+        channelize_kernel,
         grid=(coarse,),
-        out_shape=jax.ShapeDtypeStruct((dests, coarse, own // 4 * near, 8 * frames), BF16),
+        out_shape=pltpu.HBM((dests, coarse, own // 4 * near, 8 * frames), BF16),
         in_specs=[
             pl.BlockSpec(memory_space=pltpu.SMEM),
             pl.BlockSpec((2, 1, stations, half), lambda c: (0, c, 0, 0)),
             pl.BlockSpec((2, 1, own, half), lambda c: (0, c, 0, 0)),
-            pl.BlockSpec((4 * (count + 1), 8, fine), lambda c: (0, 0, 0)),
+            pl.BlockSpec((count, fine), lambda c: (0, 0)),
             pl.BlockSpec((fine, 2 * fine), lambda c: (0, 0)),
         ],
         out_specs=pl.BlockSpec((dests, 1, own // 4 * near, 8 * frames), lambda c: (0, c, 0, 0)),
         scratch_shapes=[
             pltpu.VMEM((2, own, beam * half), BF16),
-            pltpu.VMEM((2 * fine // LANES, own * 2 * frames, LANES), F32),
+            pltpu.VMEM((2 * fine // LANES, 4 * frames * PITCH, LANES), F32),
+            pltpu.VMEM((4 * (count + 1), 8, fine), F32),
         ],
         compiler_params=pltpu.CompilerParams(vmem_limit_bytes=40 * 2**20),
         name="channelize",
-    )(core.reshape(1), arranged, other, filter_tables(taps), dft_table(fine))
-
+    )(core.reshape(1), arranged, other, in_hbm(taps), in_hbm(dft_table(fine)))
+
+    spectra, codes = lax.optimization_barrier((spectra, codes))
     mixed = lax.all_to_all(spectra, ("stn", "beam"), 0, 0, tiled=True)
 
     place = jnp.stack(
-        [lax.axis_index("chan") * coarse, (lax.axis_index("stn") * beam + core) * near]
+        [
+            lax.axis_index("chan") * coarse,
+            (lax.axis_index("stn") * beam + core) * near,
+        ]
     ).astype(jnp.int32)
     total = stations * stn
+    weights = pl.pallas_call(
+        functools.partial(weight_kernel, amplitude, fine),
+        grid=(coarse,),
+        out_shape=pltpu.HBM((coarse, near, 2 * beams, total), BF16),
+        in_specs=[
+            pl.BlockSpec(memory_space=pltpu.SMEM),
+            pl.BlockSpec((stn, 4, stations // 4, beams), lambda c: (0, 0, 0, 0)),
+        ],
+        out_specs=pl.BlockSpec((1, near, 2 * beams, total), lambda c: (c, 0, 0, 0)),
+        scratch_shapes=[pltpu.VMEM((total, beams), jnp.int32)],
+        compiler_params=pltpu.CompilerParams(vmem_limit_bytes=24 * 2**20),
+        name="weights",
+    )(place, codes)
     formed = pl.pallas_call(
-        functools.partial(beam_kernel, amplitude, fine),
+        beam_kernel,
         grid=(coarse,),
         out_shape=jax.ShapeDtypeStruct((beams, coarse, near, LANES), BF16),
         in_specs=[
-            pl.BlockSpec(memory_space=pltpu.SMEM),
-            pl.BlockSpec((stn, 4, stations // 4, beams), lambda c: (0, 0, 0, 0)),
+            pl.BlockSpec((1, near, 2 * beams, total), lambda c: (c, 0, 0, 0)),
             pl.BlockSpec((dests, 1, own // 4 * near, 8 * frames), lambda c: (0, c, 0, 0)),
         ],
         out_specs=pl.BlockSpec((beams, 1, near, LANES), lambda c: (0, c, 0, 0)),
         scratch_shapes=[
-            pltpu.VMEM((total, beams), jnp.int32),
-            pltpu.VMEM((3, total // 4 * near, LANES), F32),
-            pltpu.VMEM((near, 2 * beams, total), BF16),
-            pltpu.VMEM((beams * near, LANES), F32),
-        ],
-        compiler_params=pltpu.CompilerParams(vmem_limit_bytes=40 * 2**20),
+            pltpu.VMEM((3, total // 4 * PITCH, LANES), F32),
+            pltpu.VMEM((beams * PITCH, LANES), F32),
+        ],
+        compiler_params=pltpu.CompilerParams(vmem_limit_bytes=24 * 2**20),
         name="beamform",
-    )(place, codes, mixed)
+    )(in_hbm(weights), mixed)
 
     owned = lax.all_to_all(formed, ("stn", "chan", "beam"), 0, 0, tiled=True)
     owned = owned.reshape(stn, chan, beam, coarse, near, LANES)

time: 108 us -> 90.8 us (0.84)
  blocking collectives: 70.8 us -> 24.1 us
  waiting for transfers between devices: 0.57 us -> 24.8 us
  starting transfers between devices: 9.17 us -> 15.8 us
    all_gather x1 -> x0, blocking collectives: 41.4 us -> none  [body(): codes = lax.all_gather(code, 'stn')]
    all_to_all x1, waiting for transfers between devices: 0.01 us -> 24.8 us  [body(): mixed = lax.all_to_all(spectra, ('stn', 'beam'), 0, 0, tiled=True)]
    all_to_all x0 -> x1, starting transfers between devices: none -> 6.84 us  [body(): lax.all_to_all(lax.optimization_barrier(copies), 'stn', 0, 0, tiled=True)]
    all_to_all x1, blocking collectives: 29.5 us -> 24.1 us  [body(): owned = lax.all_to_all(formed, ('stn', 'chan', 'beam'), 0, 0, tiled=True)]
    unnamed x12 -> x2, local copies, waits for them, and re-layouts: 1.43 us -> 0.01 us
    convert_element_type x1 -> x0, other arithmetic: 1.11 us -> none  [dft_table(): (jnp.sin(angle) * scale).astype(BF16)]
    pallas_call x2 -> x3, Pallas kernels: 20.3 us -> 19.6 us  [the longest x1 8.47 us: body(): pl.pallas_call(channelize_kernel, grid=(coarse,), out_shape=pltpu.HBM((de...]
  transfers between devices with their start and end apart: 2 -> 3, of which waited for: 1 -> 1; matrix products, arithmetic and copies ran while one was open for 1% -> 2% of each run, Pallas kernels for 0% -> 16%
where the time goes in v2:
time: 90.8 us; the launch traced here: 90.4 us
  waiting for transfers between devices  24.8 us (27%)
  blocking collectives  24.1 us (27%)
  Pallas kernels  21.7 us (24%)
  starting transfers between devices  15.8 us (17%)
  local copies, waits for them, and re-layouts  3 us (3%)
    all_to_all x1, waiting for transfers between devices, body(): mixed = lax.all_to_all(spectra, ('stn', 'beam'), 0, 0, tiled=True)  24.8 us
    all_to_all x1, blocking collectives, body(): owned = lax.all_to_all(formed, ('stn', 'chan', 'beam'), 0, 0, tiled=True)  24.1 us
    pallas_call x1, Pallas kernels, body(): pl.pallas_call(channelize_kernel, grid=(coarse,), out_shape=pltpu.HBM((de...  8.47 us
    all_to_all x1, starting transfers between devices, body(): mixed = lax.all_to_all(spectra, ('stn', 'beam'), 0, 0, tiled=True)  7.51 us
    all_to_all x1, starting transfers between devices, body(): lax.all_to_all(lax.optimization_barrier(copies), 'stn', 0, 0, tiled=True)  6.84 us
    pallas_call x1, Pallas kernels, body(): pl.pallas_call(functools.partial(weight_kernel, amplitude, fine), grid=(c...  5.92 us
    pallas_call x1, Pallas kernels, body(): pl.pallas_call(beam_kernel, grid=(coarse,), out_shape=jax.ShapeDtypeStruc...  5.25 us
    dynamic_slice x1, local copies, waits for them, and re-layouts, body(): away = lax.dynamic_slice_in_dim(arranged, (1 - core) * own, own, 2)  2.27 us
  transfers between devices with their start and end apart: 3, of which 1 were waited for; matrix products, arithmetic and copies ran while one was open for 2% of the time, Pallas kernels for 16%

profile of v2, /device:TPU:1, one launch (start us, length us, event | category | flops | bytes accessed | tf_op | source)
XLA Modules:
  0.0 90.4 jit_solution(18335708572456057213)
XLA Ops:
  0.0 0.0 copy-start
  0.0 2.3 %dynamic-slice_bitcast_fusion = bf16[2,3,16,4608]{3,2,1,0:T(8,128)(2,1)} fusion(bf16[2,32,3,4608]{3,1,2,0:T(8,128)(2,1)} %param.6, s32[]{:T(128)S(6)} %select_n.7), kind=kLoop, calls=%fused_computation | loop fusion | bytes 1769476 | tf_op jit(solution)/shard_map/dynamic_slice | solution.py:247
  2.3 1.4 %collective-permute-start = (bf16[2,3,16,4608]{3,2,1,0:T(8,128)(2,1)}, bf16[2,3,16,4608]{3,2,1,0:T(8,128)(2,1)S(1)}, u32[]{:S(2)}, u32[]{:S(2)}) collective-permute-start(bf16[2,3,16,4608]{3,2,1,0:T(8,128)(2,1)} %dynamic-slice_bitcast_fusion), channel_id=1, source_target_pairs={{0,1},{1,0},{2,3},{3,2},{4,5},{5,4},{6,7},{7,6},{8,9},{9,8},{10,11... | collective-permute-start | bytes 2654216 | tf_op jit(solution)/shard_map/ppermute | solution.py:248
  3.7 0.8 bitcast_select_fusion
  4.5 0.7 broadcast_in_dim.10
  5.2 6.8 %all-to-all-start = ((s32[16,4,8,128]{3,2,1,0:T(8,128)}), s32[16,4,8,128]{3,2,1,0:T(8,128)S(1)}, u32[]{:S(2)}, u32[]{:S(2)}) async-start(s32[16,4,8,128]{3,2,1,0:T(8,128)} %broadcast_in_dim.10), calls=%async_computation | async-start | bytes 524288 | tf_op jit(solution)/shard_map/all_to_all | solution.py:253
  12.1 0.0 collective-permute-done.other_ref
  12.1 0.0 copy-done
  12.1 8.5 %channelize.1 = bf16[32,3,32,384]{3,2,1,0:T(8,128)(2,1)} custom-call(s32[1]{0:T(128)} %bitcast.2.core_ref, bf16[2,3,32,4608]{3,2,1,0:T(8,128)(2,1)S(1)} %bitcast.13, bf16[2,3,16,4608]{3,2,1,0:T(8,128)(2,1)S(1)} %collective-permute-done.other_ref, f32[16,256]{1,0:T(8,128)} %prototype_ref.1, bf16[256,512]{1,0:T(8,128)(2,1)} %constant.31.clone.dft_ref), custom_call_target="tpu_custom_call" | custom-call | tf_op jit(solution)/shard_map/channelize/pallas_call | solution.py:255
  20.6 0.0 all-to-all-done.code_ref
  20.6 7.5 %all-to-all-start.1 = ((bf16[32,3,32,384]{3,2,1,0:T(8,128)(2,1)}), bf16[32,3,32,384]{3,2,1,0:T(8,128)(2,1)S(1)}, u32[]{:S(2)}, u32[]{:S(2)}) async-start(bf16[32,3,32,384]{3,2,1,0:T(8,128)(2,1)} %channelize.1), calls=%async_computation.1 | async-start | bytes 4718592 | tf_op jit(solution)/shard_map/all_to_all | solution.py:277
  28.1 0.1 pad_add_fusion.place_ref
  28.2 5.9 %weights.1.weight_ref = bf16[3,8,256,512]{3,2,1,0:T(8,128)(2,1)} custom-call(s32[2]{0:T(128)S(1)} %pad_add_fusion.place_ref, s32[16,4,8,128]{3,2,1,0:T(8,128)S(1)} %all-to-all-done.code_ref), custom_call_target="tpu_custom_call" | custom-call | tf_op jit(solution)/shard_map/weights/pallas_call | solution.py:286
  34.1 24.8 %all-to-all-done.1.data_ref = bf16[32,3,32,384]{3,2,1,0:T(8,128)(2,1)S(1)} async-done(((bf16[32,3,32,384]{3,2,1,0:T(8,128)(2,1)}), bf16[32,3,32,384]{3,2,1,0:T(8,128)(2,1)S(1)}, u32[]{:S(2)}, u32[]{:S(2)}) %all-to-all-start.1) | async-done | bytes 2359328 | tf_op jit(solution)/shard_map/all_to_all | solution.py:277
  58.9 5.2 %beamform.1 = bf16[128,3,8,128]{3,2,1,0:T(8,128)(2,1)S(1)} custom-call(bf16[3,8,256,512]{3,2,1,0:T(8,128)(2,1)} %weights.1.weight_ref, bf16[32,3,32,384]{3,2,1,0:T(8,128)(2,1)S(1)} %all-to-all-done.1.data_ref), custom_call_target="tpu_custom_call" | custom-call | tf_op jit(solution)/shard_map/beamform/pallas_call | solution.py:299
  64.1 24.1 %all_to_all.15 = bf16[128,3,8,128]{3,2,1,0:T(8,128)(2,1)S(1)} all-to-all(bf16[128,3,8,128]{3,2,1,0:T(8,128)(2,1)S(1)} %beamform.1), channel_id=1, replica_groups=mesh['stn'=16,'chan'=4,'beam'=2] {'stn','chan','beam'}, dimensions={0} | all-to-all | bytes 1572864 | tf_op jit(solution)/shard_map/all_to_all | solution.py:316
  88.3 2.1 %order.1 = f32[1,2,12,48,256]{4,3,2,1,0:T(8,128)} custom-call(bf16[16,4,2,3,8,128]{5,4,3,2,1,0:T(8,128)(2,1)S(1)} %bitcast.14), custom_call_target="tpu_custom_call" | custom-call | tf_op jit(solution)/shard_map/order/pallas_call | solution.py:318
  (1 shorter events, 0.0 us)
Async XLA Ops:
  0.0 12.1 %copy-start = (bf16[2,32,3,4608]{3,1,2,0:T(8,128)(2,1)S(1)}, bf16[2,32,3,4608]{3,1,2,0:T(8,128)(2,1)}, u32[]{:S(2)}) copy-start(bf16[2,32,3,4608]{3,1,2,0:T(8,128)(2,1)} %param.6) | copy-start | bytes 5308420
  2.3 9.8 %collective-permute-start = (bf16[2,3,16,4608]{3,2,1,0:T(8,128)(2,1)}, bf16[2,3,16,4608]{3,2,1,0:T(8,128)(2,1)S(1)}, u32[]{:S(2)}, u32[]{:S(2)}) collective-permute-start(bf16[2,3,16,4608]{3,2,1,0:T(8,128)(2,1)} %dynamic-slice_bitcast_fusion), channel_id=1, source_target_pairs={{0,1},{1,0},{2,3},{3,2},{4,5},{5,4},{6,7},{7,6},{8,9},{9,8},{10,11... | collective-permute-start | bytes 2654216 | tf_op jit(solution)/shard_map/ppermute | solution.py:248
  5.2 15.4 %all-to-all-start = ((s32[16,4,8,128]{3,2,1,0:T(8,128)}), s32[16,4,8,128]{3,2,1,0:T(8,128)S(1)}, u32[]{:S(2)}, u32[]{:S(2)}) async-start(s32[16,4,8,128]{3,2,1,0:T(8,128)} %broadcast_in_dim.10), calls=%async_computation | async-start | bytes 524288 | tf_op jit(solution)/shard_map/all_to_all | solution.py:253
  20.6 38.3 %all-to-all-start.1 = ((bf16[32,3,32,384]{3,2,1,0:T(8,128)(2,1)}), bf16[32,3,32,384]{3,2,1,0:T(8,128)(2,1)S(1)}, u32[]{:S(2)}, u32[]{:S(2)}) async-start(bf16[32,3,32,384]{3,2,1,0:T(8,128)(2,1)} %channelize.1), calls=%async_computation.1 | async-start | bytes 4718592 | tf_op jit(solution)/shard_map/all_to_all | solution.py:277

commit v3 on v2

--- a/solution.py
+++ b/solution.py
@@ -50,13 +50,27 @@
 
 
 def channelize_kernel(
-    core_ref, own_ref, other_ref, prototype_ref, dft_ref, out_ref, x_ref, z_ref, taps_ref
+    core_ref,
+    sub_ref,
+    own_ref,
+    other_ref,
+    prototype_ref,
+    dft_ref,
+    delay_ref,
+    out_ref,
+    x_ref,
+    z_ref,
+    taps_ref,
 ):
     count = prototype_ref.shape[0]
 
     @pl.when(pl.program_id(0) == 0)
     def _():
         fill_filter_tables(prototype_ref, taps_ref)
+        last = out_ref.shape[1] - 1
+        code = steering_unit(core_ref[0] * 16, sub_ref, delay_ref)
+        for dest in range(out_ref.shape[0]):
+            out_ref[dest, last] = code
 
     half = own_ref.shape[-1]
     fine = taps_ref.shape[-1]
@@ -130,7 +144,33 @@
             )
             found = lax.dot_general(table, operand, NT, preferred_element_type=F32)
             results.append(found.reshape(dests, fine // dests, 4 * rows))
-        out_ref[:, 0, pl.ds(16 * pair, 16), :] = jnp.concatenate(results, axis=1).astype(BF16)
+        for index, result in enumerate(results):
+            unit = 4 * pl.program_id(0) + 2 * pair + index
+            out_ref[:, unit] = result.astype(BF16)
+
+
+def steering_unit(first, sub_ref, delay_ref):
+    row = lax.broadcasted_iota(jnp.int32, (8, LANES), 0)
+    left = lax.broadcasted_iota(jnp.int32, (8, LANES), 1) < LANES // 2
+    tiles = []
+    subs = jnp.zeros((8, LANES), jnp.int32)
+    for side in range(2):
+        pieces = []
+        for member in (2 * side, 2 * side + 1):
+            pieces.append(delay_ref[pl.ds(first + member, 4, stride=4), :])
+            for quad in range(4):
+                chosen = (row == (member % 2) * 4 + quad) & (left == (side == 0))
+                subs = jnp.where(chosen, sub_ref[first + 4 * quad + member], subs)
+        delay = jnp.concatenate(pieces, axis=0)
+        tiles.append(lax.shift_left(128 + (delay & 127), lax.shift_right_logical(delay, 7)))
+    return jnp.concatenate(tiles + [subs], axis=1).astype(F32).astype(BF16)
+
+
+def delay_of(code):
+    high = jnp.zeros_like(code)
+    for power in range(8, 15):
+        high = high + (code >= 2**power).astype(jnp.int32)
+    return high * 128 + lax.shift_right_logical(code, high) - 128
 
 
 def turn_parts(turn):
@@ -147,18 +187,40 @@
     return cos_part, sin_part
 
 
-def weight_kernel(amplitude, fine, place_ref, code_ref, weight_ref, delay_ref):
-    near, rows, stations = weight_ref.shape[1:]
+def beam_kernel(
+    amplitude,
+    fine,
+    place_ref,
+    beam_sub_ref,
+    code_ref,
+    data_ref,
+    out_ref,
+    delay_ref,
+    weight_ref,
+    flat_ref,
+    sum_ref,
+):
+    near, rows, stations = weight_ref.shape
     beams = rows // 2
+    sources, quads = data_ref.shape[:2]
     depth = stations // 4
     coarse = pl.program_id(0)
 
     @pl.when(coarse == 0)
     def _():
-        width = code_ref.shape[2]
-        for index in range(code_ref.shape[0]):
-            for member in range(4):
-                delay_ref[pl.ds(member * depth + index * width, width), :] = code_ref[index, member]
+        lane = lax.broadcasted_iota(jnp.int32, (8, LANES), 1)
+        wanted = beam_sub_ref[...]
+        for source in range(sources):
+            subs = code_ref[source, 0, :, pl.ds(2 * LANES, LANES)].astype(F32)
+            turned = pltpu.roll(subs, LANES // 2, 1)
+            for side in range(2):
+                value = code_ref[source, 0, :, pl.ds(side * LANES, LANES)].astype(F32)
+                delay = delay_of(value.astype(jnp.int32))
+                sub = jnp.where((lane < LANES // 2) == (side == 0), subs, turned)
+                delay = jnp.where(sub == wanted, delay, -1)
+                for index in range(2):
+                    at = (2 * side + index) * depth + source * quads
+                    delay_ref[pl.ds(at, quads), :] = delay[index * quads : (index + 1) * quads]
 
     freq = (place_ref[0] + coarse) * fine + place_ref[1]
     strip = 32
@@ -173,27 +235,20 @@
             cos_step, sin_step = turn_parts(delay)
             real, imag = cos_part * scale, -(sin_part * scale)
             for step in range(near):
-                weight_ref[0, step, pl.ds(top, strip), lanes] = real.astype(BF16)
-                weight_ref[0, step, pl.ds(beams + top, strip), lanes] = imag.astype(BF16)
+                weight_ref[step, pl.ds(top, strip), lanes] = real.astype(BF16)
+                weight_ref[step, pl.ds(beams + top, strip), lanes] = imag.astype(BF16)
                 if step + 1 < near:
                     real, imag = (
                         real * cos_step + imag * sin_step,
                         imag * cos_step - real * sin_step,
                     )
 
-
-def beam_kernel(weight_ref, data_ref, out_ref, flat_ref, sum_ref):
-    sources = data_ref.shape[0]
-    beams = out_ref.shape[0]
-    near = out_ref.shape[2]
-    quads = data_ref.shape[2] // near
-    depth = sources * quads
     for tile in range(3):
         for source in range(sources):
-            block = data_ref[source, 0, :, pl.ds(tile * LANES, LANES)].astype(F32)
             for quad in range(quads):
+                block = data_ref[source, quad, :, pl.ds(tile * LANES, LANES)].astype(F32)
                 row = PITCH * (source * quads + quad)
-                flat_ref[tile, pl.ds(row, near), :] = block[quad * near : (quad + 1) * near]
+                flat_ref[tile, pl.ds(row, near), :] = block
     lane = lax.broadcasted_iota(jnp.int32, (depth, LANES), 1)
     lane_out = lax.broadcasted_iota(jnp.int32, (beams, LANES), 1)
     for step in range(near):
@@ -204,7 +259,7 @@
             jnp.where(lane < 64, pltpu.roll(pieces[1], 64, 1), pltpu.roll(pieces[2], 96, 1)),
         )
         operand = jnp.concatenate([piece.astype(BF16) for piece in pieces + [last]], axis=0)
-        found = lax.dot_general(weight_ref[0, step], operand, NN, preferred_element_type=F32)
+        found = lax.dot_general(weight_ref[step], operand, NN, preferred_element_type=F32)
         by_real, by_imag = found[:beams], found[beams:]
         crossed = jnp.where(lane_out < 48, -pltpu.roll(by_imag, 80, 1), pltpu.roll(by_imag, 48, 1))
         sum_ref[pl.ds(step, beams, stride=PITCH), :] = by_real + crossed
@@ -247,23 +302,23 @@
     away = lax.dynamic_slice_in_dim(arranged, (1 - core) * own, own, 2)
     other = lax.ppermute(away, "beam", [(0, 1), (1, 0)])
 
-    code = jnp.where(station_sub[:, None] == beam_sub[None, :], delays.T, -1)
-    code = code.reshape(stations // 4, 4, beams).transpose(1, 0, 2)
-    copies = jnp.broadcast_to(code, (stn,) + code.shape)
-    codes = lax.all_to_all(lax.optimization_barrier(copies), "stn", 0, 0, tiled=True)
+    quads = own // 4
+    units = coarse * quads + 1
 
     spectra = pl.pallas_call(
         channelize_kernel,
         grid=(coarse,),
-        out_shape=pltpu.HBM((dests, coarse, own // 4 * near, 8 * frames), BF16),
+        out_shape=pltpu.HBM((dests, units, near, 8 * frames), BF16),
         in_specs=[
+            pl.BlockSpec(memory_space=pltpu.SMEM),
             pl.BlockSpec(memory_space=pltpu.SMEM),
             pl.BlockSpec((2, 1, stations, half), lambda c: (0, c, 0, 0)),
             pl.BlockSpec((2, 1, own, half), lambda c: (0, c, 0, 0)),
             pl.BlockSpec((count, fine), lambda c: (0, 0)),
             pl.BlockSpec((fine, 2 * fine), lambda c: (0, 0)),
-        ],
-        out_specs=pl.BlockSpec((dests, 1, own // 4 * near, 8 * frames), lambda c: (0, c, 0, 0)),
+            pl.BlockSpec((stations, beams), lambda c: (0, 0)),
+        ],
+        out_specs=pl.BlockSpec((dests, units, near, 8 * frames), lambda c: (0, 0, 0, 0)),
         scratch_shapes=[
             pltpu.VMEM((2, own, beam * half), BF16),
             pltpu.VMEM((2 * fine // LANES, 4 * frames * PITCH, LANES), F32),
@@ -271,9 +326,16 @@
         ],
         compiler_params=pltpu.CompilerParams(vmem_limit_bytes=40 * 2**20),
         name="channelize",
-    )(core.reshape(1), arranged, other, in_hbm(taps), in_hbm(dft_table(fine)))
-
-    spectra, codes = lax.optimization_barrier((spectra, codes))
+    )(
+        core.reshape(1),
+        station_sub,
+        arranged,
+        other,
+        in_hbm(taps),
+        in_hbm(dft_table(fine)),
+        in_hbm(delays.T),
+    )
+
     mixed = lax.all_to_all(spectra, ("stn", "beam"), 0, 0, tiled=True)
 
     place = jnp.stack(
@@ -283,35 +345,26 @@
         ]
     ).astype(jnp.int32)
     total = stations * stn
-    weights = pl.pallas_call(
-        functools.partial(weight_kernel, amplitude, fine),
-        grid=(coarse,),
-        out_shape=pltpu.HBM((coarse, near, 2 * beams, total), BF16),
-        in_specs=[
-            pl.BlockSpec(memory_space=pltpu.SMEM),
-            pl.BlockSpec((stn, 4, stations // 4, beams), lambda c: (0, 0, 0, 0)),
-        ],
-        out_specs=pl.BlockSpec((1, near, 2 * beams, total), lambda c: (c, 0, 0, 0)),
-        scratch_shapes=[pltpu.VMEM((total, beams), jnp.int32)],
-        compiler_params=pltpu.CompilerParams(vmem_limit_bytes=24 * 2**20),
-        name="weights",
-    )(place, codes)
     formed = pl.pallas_call(
-        beam_kernel,
+        functools.partial(beam_kernel, amplitude, fine),
         grid=(coarse,),
         out_shape=jax.ShapeDtypeStruct((beams, coarse, near, LANES), BF16),
         in_specs=[
-            pl.BlockSpec((1, near, 2 * beams, total), lambda c: (c, 0, 0, 0)),
-            pl.BlockSpec((dests, 1, own // 4 * near, 8 * frames), lambda c: (0, c, 0, 0)),
+            pl.BlockSpec(memory_space=pltpu.SMEM),
+            pl.BlockSpec((1, beams), lambda c: (0, 0)),
+            pl.BlockSpec((dests, 1, near, 8 * frames), lambda c: (0, units - 1, 0, 0)),
+            pl.BlockSpec((dests, quads, near, 8 * frames), lambda c: (0, c, 0, 0)),
         ],
         out_specs=pl.BlockSpec((beams, 1, near, LANES), lambda c: (0, c, 0, 0)),
         scratch_shapes=[
+            pltpu.VMEM((total, beams), jnp.int32),
+            pltpu.VMEM((near, 2 * beams, total), BF16),
             pltpu.VMEM((3, total // 4 * PITCH, LANES), F32),
             pltpu.VMEM((beams * PITCH, LANES), F32),
         ],
-        compiler_params=pltpu.CompilerParams(vmem_limit_bytes=24 * 2**20),
+        compiler_params=pltpu.CompilerParams(vmem_limit_bytes=40 * 2**20),
         name="beamform",
-    )(in_hbm(weights), mixed)
+    )(place, beam_sub.astype(F32).reshape(1, beams), mixed, mixed)
 
     owned = lax.all_to_all(formed, ("stn", "chan", "beam"), 0, 0, tiled=True)
     owned = owned.reshape(stn, chan, beam, coarse, near, LANES)

time: 90.8 us -> 88.7 us (0.977)
  waiting for transfers between devices: 24.8 us -> 34.8 us
  starting transfers between devices: 15.8 us -> 9.19 us
  Pallas kernels: 21.7 us -> 18.9 us
  local copies, waits for them, and re-layouts: 3 us -> 1.37 us
    all_to_all x1, waiting for transfers between devices: 24.8 us -> 32.8 us  [body(): mixed = lax.all_to_all(spectra, ('stn', 'beam'), 0, 0, tiled=True)]
    all_to_all x1 -> x0, starting transfers between devices: 6.84 us -> none  [body(): lax.all_to_all(lax.optimization_barrier(copies), 'stn', 0, 0, tiled=True)]
    pallas_call x2 -> x1, Pallas kernels: 11.2 us -> 7.84 us  [body(): pl.pallas_call(functools.partial(beam_kernel, amplitude, fine), grid=(coa...]
    ppermute x1, waiting for transfers between devices: 0.01 us -> 2.05 us  [body(): other = lax.ppermute(away, 'beam', [(0, 1), (1, 0)])]
    dynamic_slice x1, local copies, waits for them, and re-layouts: 2.27 us -> 1.36 us  [body(): away = lax.dynamic_slice_in_dim(arranged, (1 - core) * own, own, 2)]
  transfers between devices with their start and end apart: 3 -> 2, of which waited for: 1 -> 2; matrix products, arithmetic and copies ran while one was open for 2% -> 0% of each run, Pallas kernels for 16% -> 0%
where the time goes in v3:
time: 88.7 us; the launch traced here: 88.5 us
  waiting for transfers between devices  34.8 us (39%)
  blocking collectives  24.1 us (27%)
  Pallas kernels  18.9 us (21%)
  starting transfers between devices  9.19 us (10%)
  local copies, waits for them, and re-layouts  1.37 us (2%)
    all_to_all x1, waiting for transfers between devices, body(): mixed = lax.all_to_all(spectra, ('stn', 'beam'), 0, 0, tiled=True)  32.8 us
    all_to_all x1, blocking collectives, body(): owned = lax.all_to_all(formed, ('stn', 'chan', 'beam'), 0, 0, tiled=True)  24.1 us
    pallas_call x1, Pallas kernels, body(): pl.pallas_call(channelize_kernel, grid=(coarse,), out_shape=pltpu.HBM((de...  8.99 us
    pallas_call x1, Pallas kernels, body(): pl.pallas_call(functools.partial(beam_kernel, amplitude, fine), grid=(coa...  7.84 us
    all_to_all x1, starting transfers between devices, body(): mixed = lax.all_to_all(spectra, ('stn', 'beam'), 0, 0, tiled=True)  7.69 us
    pallas_call x1, Pallas kernels, body(): pl.pallas_call(order_kernel, grid=(chan,), out_shape=jax.ShapeDtypeStruct...  2.11 us
    ppermute x1, waiting for transfers between devices, body(): other = lax.ppermute(away, 'beam', [(0, 1), (1, 0)])  2.05 us
  transfers between devices with their start and end apart: 2, of which 2 were waited for; matrix products, arithmetic and copies ran while one was open for 0% of the time, Pallas kernels for 0%

profile of v3, /device:TPU:1, one launch (start us, length us, event | category | flops | bytes accessed | tf_op | source)
XLA Modules:
  0.0 88.5 jit_solution(9834148620636344563)
XLA Ops:
  0.0 0.0 copy-start
  0.0 0.0 copy-start.1
  0.0 1.4 %dynamic-slice_bitcast_fusion = bf16[2,3,16,4608]{3,2,1,0:T(8,128)(2,1)S(1)} fusion(bf16[2,32,3,4608]{3,1,2,0:T(8,128)(2,1)} %param.6, s32[]{:T(128)S(6)} %select_n.3), kind=kLoop, calls=%fused_computation | loop fusion | bytes 1769476 | tf_op jit(solution)/shard_map/dynamic_slice | solution.py:302
  1.4 1.5 %collective-permute-start = (bf16[2,3,16,4608]{3,2,1,0:T(8,128)(2,1)S(1)}, bf16[2,3,16,4608]{3,2,1,0:T(8,128)(2,1)S(1)}, u32[]{:S(2)}, u32[]{:S(2)}) collective-permute-start(bf16[2,3,16,4608]{3,2,1,0:T(8,128)(2,1)S(1)} %dynamic-slice_bitcast_fusion), channel_id=1, source_target_pairs={{0,1},{1,0},{2,3},{3,2},{4,5},{5,4},{6,7},{7,6},{8,9},{9,8},{10,11... | collective-permute-start | bytes 2654216 | tf_op jit(solution)/shard_map/ppermute | solution.py:303
  2.9 2.1 %collective-permute-done.other_ref = bf16[2,3,16,4608]{3,2,1,0:T(8,128)(2,1)S(1)} collective-permute-done((bf16[2,3,16,4608]{3,2,1,0:T(8,128)(2,1)S(1)}, bf16[2,3,16,4608]{3,2,1,0:T(8,128)(2,1)S(1)}, u32[]{:S(2)}, u32[]{:S(2)}) %collective-permute-start) | collective-permute-done | bytes 884768 | tf_op jit(solution)/shard_map/ppermute | solution.py:303
  4.9 0.0 copy-done
  4.9 0.0 copy-done.1
  4.9 9.0 %channelize.1 = bf16[32,13,8,384]{3,2,1,0:T(8,128)(2,1)} custom-call(s32[1]{0:T(128)} %bitcast.3.core_ref, s32[32]{0:T(128)S(1)} %copy-done.1, bf16[2,3,32,4608]{3,2,1,0:T(8,128)(2,1)S(1)} %bitcast.10, bf16[2,3,16,4608]{3,2,1,0:T(8,128)(2,1)S(1)} %collective-permute-done.other_ref, f32[16,256]{1,0:T(8,128)} %prototype_ref.1, ...), custom_call_target="tpu_custom_call" | custom-call | tf_op jit(solution)/shard_map/channelize/pallas_call | solution.py:308
  13.9 0.0 copy-start.2
  13.9 7.7 %all-to-all-start = ((bf16[32,13,8,384]{3,2,1,0:T(8,128)(2,1)}), bf16[32,13,8,384]{3,2,1,0:T(8,128)(2,1)S(1)}, u32[]{:S(2)}, u32[]{:S(2)}) async-start(bf16[32,13,8,384]{3,2,1,0:T(8,128)(2,1)} %channelize.1), calls=%async_computation | async-start | bytes 5111808 | tf_op jit(solution)/shard_map/all_to_all | solution.py:339
  21.6 0.1 pad_add_fusion.place_ref
  21.7 0.0 copy-done.2
  21.7 32.8 %all-to-all-done.code_ref.data_ref = bf16[32,13,8,384]{3,2,1,0:T(8,128)(2,1)S(1)} async-done(((bf16[32,13,8,384]{3,2,1,0:T(8,128)(2,1)}), bf16[32,13,8,384]{3,2,1,0:T(8,128)(2,1)S(1)}, u32[]{:S(2)}, u32[]{:S(2)}) %all-to-all-start) | async-done | bytes 2555936 | tf_op jit(solution)/shard_map/all_to_all | solution.py:339
  54.5 7.8 %beamform.1 = bf16[128,3,8,128]{3,2,1,0:T(8,128)(2,1)S(1)} custom-call(s32[2]{0:T(128)S(1)} %pad_add_fusion.place_ref, f32[1,128]{1,0:T(1,128)S(1)} %convert_bitcast_fusion.beam_sub_ref, bf16[32,13,8,384]{3,2,1,0:T(8,128)(2,1)S(1)} %all-to-all-done.code_ref.data_ref, bf16[32,13,8,384]{3,2,1,0:T(8,128)(2,1)S(1)} %all-to-all-done.code_ref.data_ref), custom_call_target="tpu_custom_call" | custom-call | tf_op jit(solution)/shard_map/beamform/pallas_call | solution.py:348
  62.3 24.1 %all_to_all.10 = bf16[128,3,8,128]{3,2,1,0:T(8,128)(2,1)S(1)} all-to-all(bf16[128,3,8,128]{3,2,1,0:T(8,128)(2,1)S(1)} %beamform.1), channel_id=1, replica_groups=mesh['stn'=16,'chan'=4,'beam'=2] {'stn','chan','beam'}, dimensions={0} | all-to-all | bytes 1572864 | tf_op jit(solution)/shard_map/all_to_all | solution.py:369
  86.4 2.1 %order.1 = f32[1,2,12,48,256]{4,3,2,1,0:T(8,128)} custom-call(bf16[16,4,2,3,8,128]{5,4,3,2,1,0:T(8,128)(2,1)S(1)} %bitcast.11), custom_call_target="tpu_custom_call" | custom-call | tf_op jit(solution)/shard_map/order/pallas_call | solution.py:371
  (1 shorter events, 0.0 us)
Async XLA Ops:
  0.0 4.9 %copy-start = (bf16[2,32,3,4608]{3,1,2,0:T(8,128)(2,1)S(1)}, bf16[2,32,3,4608]{3,1,2,0:T(8,128)(2,1)}, u32[]{:S(2)}) copy-start(bf16[2,32,3,4608]{3,1,2,0:T(8,128)(2,1)} %param.6) | copy-start | bytes 5308420
  0.0 4.9 %copy-start.1 = (s32[32]{0:T(128)S(1)}, s32[32]{0:T(128)}, u32[]{:S(2)}) copy-start(s32[32]{0:T(128)} %sub_ref.1) | copy-start | bytes 388
  1.4 3.6 %collective-permute-start = (bf16[2,3,16,4608]{3,2,1,0:T(8,128)(2,1)S(1)}, bf16[2,3,16,4608]{3,2,1,0:T(8,128)(2,1)S(1)}, u32[]{:S(2)}, u32[]{:S(2)}) collective-permute-start(bf16[2,3,16,4608]{3,2,1,0:T(8,128)(2,1)S(1)} %dynamic-slice_bitcast_fusion), channel_id=1, source_target_pairs={{0,1},{1,0},{2,3},{3,2},{4,5},{5,4},{6,7},{7,6},{8,9},{9,8},{10,11... | collective-permute-start | bytes 2654216 | tf_op jit(solution)/shard_map/ppermute | solution.py:303
  13.9 7.8 %copy-start.2 = (s32[128]{0:T(128)S(1)}, s32[128]{0:T(128)}, u32[]{:S(2)}) copy-start(s32[128]{0:T(128)} %param.10) | copy-start | bytes 1540
  13.9 40.5 %all-to-all-start = ((bf16[32,13,8,384]{3,2,1,0:T(8,128)(2,1)}), bf16[32,13,8,384]{3,2,1,0:T(8,128)(2,1)S(1)}, u32[]{:S(2)}, u32[]{:S(2)}) async-start(bf16[32,13,8,384]{3,2,1,0:T(8,128)(2,1)} %channelize.1), calls=%async_computation | async-start | bytes 5111808 | tf_op jit(solution)/shard_map/all_to_all | solution.py:339

commit v4 on v3

--- a/solution.py
+++ b/solution.py
@@ -196,6 +196,7 @@
     data_ref,
     out_ref,
     delay_ref,
+    state_ref,
     weight_ref,
     flat_ref,
     sum_ref,
@@ -222,18 +223,32 @@
                     at = (2 * side + index) * depth + source * quads
                     delay_ref[pl.ds(at, quads), :] = delay[index * quads : (index + 1) * quads]
 
-    freq = (place_ref[0] + coarse) * fine + place_ref[1]
-    strip = 32
+    strip = 16
+
+    @pl.when(coarse == 0)
+    def _():
+        freq = place_ref[0] * fine + place_ref[1]
+        for member in range(4):
+            lanes = pl.ds(member * depth, depth)
+            turned = jnp.transpose(delay_ref[lanes, :].astype(F32)).astype(jnp.int32)
+            for top in range(0, beams, strip):
+                delay = turned[top : top + strip]
+                scale = jnp.where(delay >= 0, amplitude, 0.0).astype(F32)
+                delay = jnp.maximum(delay, 0)
+                cos_part, sin_part = turn_parts((delay * freq) & 65535)
+                parts = (cos_part * scale, -(sin_part * scale))
+                parts = parts + turn_parts(delay) + turn_parts((delay * fine) & 65535)
+                for index, part in enumerate(parts):
+                    state_ref[index, pl.ds(top, strip), lanes] = part
+
     for member in range(4):
         lanes = pl.ds(member * depth, depth)
-        turned = jnp.transpose(delay_ref[lanes, :].astype(F32)).astype(jnp.int32)
         for top in range(0, beams, strip):
-            delay = turned[top : top + strip]
-            scale = jnp.where(delay >= 0, amplitude, 0.0).astype(F32)
-            delay = jnp.maximum(delay, 0)
-            cos_part, sin_part = turn_parts((delay * freq) & 65535)
-            cos_step, sin_step = turn_parts(delay)
-            real, imag = cos_part * scale, -(sin_part * scale)
+            here = (pl.ds(top, strip), lanes)
+            first_real, first_imag, cos_step, sin_step, cos_jump, sin_jump = [
+                state_ref[index, here[0], here[1]] for index in range(6)
+            ]
+            real, imag = first_real, first_imag
             for step in range(near):
                 weight_ref[step, pl.ds(top, strip), lanes] = real.astype(BF16)
                 weight_ref[step, pl.ds(beams + top, strip), lanes] = imag.astype(BF16)
@@ -242,6 +257,8 @@
                         real * cos_step + imag * sin_step,
                         imag * cos_step - real * sin_step,
                     )
+            state_ref[0, here[0], here[1]] = first_real * cos_jump + first_imag * sin_jump
+            state_ref[1, here[0], here[1]] = first_imag * cos_jump - first_real * sin_jump
 
     for tile in range(3):
         for source in range(sources):
@@ -358,6 +375,7 @@
         out_specs=pl.BlockSpec((beams, 1, near, LANES), lambda c: (0, c, 0, 0)),
         scratch_shapes=[
             pltpu.VMEM((total, beams), jnp.int32),
+            pltpu.VMEM((6, beams, total), F32),
             pltpu.VMEM((near, 2 * beams, total), BF16),
             pltpu.VMEM((3, total // 4 * PITCH, LANES), F32),
             pltpu.VMEM((beams * PITCH, LANES), F32),

time: 88.7 us -> 88.4 us (level)
  no operation moved by 1% of the time
where the time goes in v4:
time: 88.4 us; the launch traced here: 88.2 us
  waiting for transfers between devices  34.8 us (39%)
  blocking collectives  24.1 us (27%)
  Pallas kernels  18.6 us (21%)
  starting transfers between devices  9.19 us (10%)
  local copies, waits for them, and re-layouts  1.37 us (2%)
    all_to_all x1, waiting for transfers between devices, body(): mixed = lax.all_to_all(spectra, ('stn', 'beam'), 0, 0, tiled=True)  32.8 us
    all_to_all x1, blocking collectives, body(): owned = lax.all_to_all(formed, ('stn', 'chan', 'beam'), 0, 0, tiled=True)  24.1 us
    pallas_call x1, Pallas kernels, body(): pl.pallas_call(channelize_kernel, grid=(coarse,), out_shape=pltpu.HBM((de...  8.99 us
    all_to_all x1, starting transfers between devices, body(): mixed = lax.all_to_all(spectra, ('stn', 'beam'), 0, 0, tiled=True)  7.69 us
    pallas_call x1, Pallas kernels, body(): pl.pallas_call(functools.partial(beam_kernel, amplitude, fine), grid=(coa...  7.51 us
    pallas_call x1, Pallas kernels, body(): pl.pallas_call(order_kernel, grid=(chan,), out_shape=jax.ShapeDtypeStruct...  2.1 us
    ppermute x1, waiting for transfers between devices, body(): other = lax.ppermute(away, 'beam', [(0, 1), (1, 0)])  2.05 us
  transfers between devices with their start and end apart: 2, of which 2 were waited for; matrix products, arithmetic and copies ran while one was open for 0% of the time, Pallas kernels for 0%

profile of v4, /device:TPU:1, one launch (start us, length us, event | category | flops | bytes accessed | tf_op | source)
XLA Modules:
  0.0 88.2 jit_solution(4526049940744214454)
XLA Ops:
  0.0 0.0 copy-start
  0.0 0.0 copy-start.1
  0.0 1.4 %dynamic-slice_bitcast_fusion = bf16[2,3,16,4608]{3,2,1,0:T(8,128)(2,1)S(1)} fusion(bf16[2,32,3,4608]{3,1,2,0:T(8,128)(2,1)} %param.6, s32[]{:T(128)S(6)} %select_n.3), kind=kLoop, calls=%fused_computation | loop fusion | bytes 1769476 | tf_op jit(solution)/shard_map/dynamic_slice | solution.py:319
  1.4 1.5 %collective-permute-start = (bf16[2,3,16,4608]{3,2,1,0:T(8,128)(2,1)S(1)}, bf16[2,3,16,4608]{3,2,1,0:T(8,128)(2,1)S(1)}, u32[]{:S(2)}, u32[]{:S(2)}) collective-permute-start(bf16[2,3,16,4608]{3,2,1,0:T(8,128)(2,1)S(1)} %dynamic-slice_bitcast_fusion), channel_id=1, source_target_pairs={{0,1},{1,0},{2,3},{3,2},{4,5},{5,4},{6,7},{7,6},{8,9},{9,8},{10,11... | collective-permute-start | bytes 2654216 | tf_op jit(solution)/shard_map/ppermute | solution.py:320
  2.9 2.1 %collective-permute-done.other_ref = bf16[2,3,16,4608]{3,2,1,0:T(8,128)(2,1)S(1)} collective-permute-done((bf16[2,3,16,4608]{3,2,1,0:T(8,128)(2,1)S(1)}, bf16[2,3,16,4608]{3,2,1,0:T(8,128)(2,1)S(1)}, u32[]{:S(2)}, u32[]{:S(2)}) %collective-permute-start) | collective-permute-done | bytes 884768 | tf_op jit(solution)/shard_map/ppermute | solution.py:320
  4.9 0.0 copy-done
  4.9 0.0 copy-done.1
  4.9 9.0 %channelize.1 = bf16[32,13,8,384]{3,2,1,0:T(8,128)(2,1)} custom-call(s32[1]{0:T(128)} %bitcast.3.core_ref, s32[32]{0:T(128)S(1)} %copy-done.1, bf16[2,3,32,4608]{3,2,1,0:T(8,128)(2,1)S(1)} %bitcast.10, bf16[2,3,16,4608]{3,2,1,0:T(8,128)(2,1)S(1)} %collective-permute-done.other_ref, f32[16,256]{1,0:T(8,128)} %prototype_ref.1, ...), custom_call_target="tpu_custom_call" | custom-call | tf_op jit(solution)/shard_map/channelize/pallas_call | solution.py:325
  13.9 0.0 copy-start.2
  13.9 7.7 %all-to-all-start = ((bf16[32,13,8,384]{3,2,1,0:T(8,128)(2,1)}), bf16[32,13,8,384]{3,2,1,0:T(8,128)(2,1)S(1)}, u32[]{:S(2)}, u32[]{:S(2)}) async-start(bf16[32,13,8,384]{3,2,1,0:T(8,128)(2,1)} %channelize.1), calls=%async_computation | async-start | bytes 5111808 | tf_op jit(solution)/shard_map/all_to_all | solution.py:356
  21.6 0.1 pad_add_fusion.place_ref
  21.7 0.0 copy-done.2
  21.7 32.8 %all-to-all-done.code_ref.data_ref = bf16[32,13,8,384]{3,2,1,0:T(8,128)(2,1)S(1)} async-done(((bf16[32,13,8,384]{3,2,1,0:T(8,128)(2,1)}), bf16[32,13,8,384]{3,2,1,0:T(8,128)(2,1)S(1)}, u32[]{:S(2)}, u32[]{:S(2)}) %all-to-all-start) | async-done | bytes 2555936 | tf_op jit(solution)/shard_map/all_to_all | solution.py:356
  54.5 7.5 %beamform.1 = bf16[128,3,8,128]{3,2,1,0:T(8,128)(2,1)S(1)} custom-call(s32[2]{0:T(128)S(1)} %pad_add_fusion.place_ref, f32[1,128]{1,0:T(1,128)S(1)} %convert_bitcast_fusion.beam_sub_ref, bf16[32,13,8,384]{3,2,1,0:T(8,128)(2,1)S(1)} %all-to-all-done.code_ref.data_ref, bf16[32,13,8,384]{3,2,1,0:T(8,128)(2,1)S(1)} %all-to-all-done.code_ref.data_ref), custom_call_target="tpu_custom_call" | custom-call | tf_op jit(solution)/shard_map/beamform/pallas_call | solution.py:365
  62.0 24.1 %all_to_all.10 = bf16[128,3,8,128]{3,2,1,0:T(8,128)(2,1)S(1)} all-to-all(bf16[128,3,8,128]{3,2,1,0:T(8,128)(2,1)S(1)} %beamform.1), channel_id=1, replica_groups=mesh['stn'=16,'chan'=4,'beam'=2] {'stn','chan','beam'}, dimensions={0} | all-to-all | bytes 1572864 | tf_op jit(solution)/shard_map/all_to_all | solution.py:387
  86.1 2.1 %order.1 = f32[1,2,12,48,256]{4,3,2,1,0:T(8,128)} custom-call(bf16[16,4,2,3,8,128]{5,4,3,2,1,0:T(8,128)(2,1)S(1)} %bitcast.11), custom_call_target="tpu_custom_call" | custom-call | tf_op jit(solution)/shard_map/order/pallas_call | solution.py:389
  (1 shorter events, 0.0 us)
Async XLA Ops:
  0.0 4.9 %copy-start = (bf16[2,32,3,4608]{3,1,2,0:T(8,128)(2,1)S(1)}, bf16[2,32,3,4608]{3,1,2,0:T(8,128)(2,1)}, u32[]{:S(2)}) copy-start(bf16[2,32,3,4608]{3,1,2,0:T(8,128)(2,1)} %param.6) | copy-start | bytes 5308420
  0.0 4.9 %copy-start.1 = (s32[32]{0:T(128)S(1)}, s32[32]{0:T(128)}, u32[]{:S(2)}) copy-start(s32[32]{0:T(128)} %sub_ref.1) | copy-start | bytes 388
  1.4 3.6 %collective-permute-start = (bf16[2,3,16,4608]{3,2,1,0:T(8,128)(2,1)S(1)}, bf16[2,3,16,4608]{3,2,1,0:T(8,128)(2,1)S(1)}, u32[]{:S(2)}, u32[]{:S(2)}) collective-permute-start(bf16[2,3,16,4608]{3,2,1,0:T(8,128)(2,1)S(1)} %dynamic-slice_bitcast_fusion), channel_id=1, source_target_pairs={{0,1},{1,0},{2,3},{3,2},{4,5},{5,4},{6,7},{7,6},{8,9},{9,8},{10,11... | collective-permute-start | bytes 2654216 | tf_op jit(solution)/shard_map/ppermute | solution.py:320
  13.9 7.8 %copy-start.2 = (s32[128]{0:T(128)S(1)}, s32[128]{0:T(128)}, u32[]{:S(2)}) copy-start(s32[128]{0:T(128)} %param.10) | copy-start | bytes 1540
  13.9 40.5 %all-to-all-start = ((bf16[32,13,8,384]{3,2,1,0:T(8,128)(2,1)}), bf16[32,13,8,384]{3,2,1,0:T(8,128)(2,1)S(1)}, u32[]{:S(2)}, u32[]{:S(2)}) async-start(bf16[32,13,8,384]{3,2,1,0:T(8,128)(2,1)} %channelize.1), calls=%async_computation | async-start | bytes 5111808 | tf_op jit(solution)/shard_map/all_to_all | solution.py:356

commit v5 on v4

--- a/solution.py
+++ b/solution.py
@@ -325,7 +325,7 @@
     spectra = pl.pallas_call(
         channelize_kernel,
         grid=(coarse,),
-        out_shape=pltpu.HBM((dests, units, near, 8 * frames), BF16),
+        out_shape=jax.ShapeDtypeStruct((dests, units, near, 8 * frames), BF16),
         in_specs=[
             pl.BlockSpec(memory_space=pltpu.SMEM),
             pl.BlockSpec(memory_space=pltpu.SMEM),
@@ -353,14 +353,16 @@
         in_hbm(delays.T),
     )
 
-    mixed = lax.all_to_all(spectra, ("stn", "beam"), 0, 0, tiled=True)
-
     place = jnp.stack(
         [
             lax.axis_index("chan") * coarse,
             (lax.axis_index("stn") * beam + core) * near,
         ]
     ).astype(jnp.int32)
+    wanted = beam_sub.astype(F32).reshape(1, beams)
+    spectra, place, wanted = lax.optimization_barrier((spectra, place, wanted))
+    mixed = lax.all_to_all(spectra, ("stn", "beam"), 0, 0, tiled=True)
+
     total = stations * stn
     formed = pl.pallas_call(
         functools.partial(beam_kernel, amplitude, fine),
@@ -382,7 +384,7 @@
         ],
         compiler_params=pltpu.CompilerParams(vmem_limit_bytes=40 * 2**20),
         name="beamform",
-    )(place, beam_sub.astype(F32).reshape(1, beams), mixed, mixed)
+    )(place, wanted, mixed, mixed)
 
     owned = lax.all_to_all(formed, ("stn", "chan", "beam"), 0, 0, tiled=True)
     owned = owned.reshape(stn, chan, beam, coarse, near, LANES)

time: 88.4 us -> 85.8 us (0.971)
  blocking collectives: 24.1 us -> 63.6 us
  waiting for transfers between devices: 34.8 us -> 1.97 us
  starting transfers between devices: 9.19 us -> 1.5 us
  Pallas kernels: 18.6 us -> 17.1 us
    all_to_all x0 -> x1, blocking collectives: none -> 40.7 us  [body(): mixed = lax.all_to_all(spectra, ('stn', 'beam'), 0, 0, tiled=True)]
    all_to_all x1 -> x0, waiting for transfers between devices: 32.8 us -> none  [body(): mixed = lax.all_to_all(spectra, ('stn', 'beam'), 0, 0, tiled=True)]
    all_to_all x1 -> x0, starting transfers between devices: 7.69 us -> none  [body(): mixed = lax.all_to_all(spectra, ('stn', 'beam'), 0, 0, tiled=True)]
    pallas_call x1, Pallas kernels: 8.99 us -> 7.52 us  [body(): pl.pallas_call(channelize_kernel, grid=(coarse,), out_shape=jax.ShapeDtyp...]
    all_to_all x1, blocking collectives: 24.1 us -> 22.9 us  [body(): owned = lax.all_to_all(formed, ('stn', 'chan', 'beam'), 0, 0, tiled=True)]
  transfers between devices with their start and end apart: 2 -> 1, of which waited for: 2 -> 1; matrix products, arithmetic and copies ran while one was open for 0% -> 0% of each run, Pallas kernels for 0% -> 0%
where the time goes in v5:
time: 85.8 us; the launch traced here: 85.6 us
  blocking collectives  63.6 us (74%)
  Pallas kernels  17.1 us (20%)
  waiting for transfers between devices  1.97 us (2%)
  starting transfers between devices  1.5 us (2%)
  local copies, waits for them, and re-layouts  1.37 us (2%)
    all_to_all x1, blocking collectives, body(): mixed = lax.all_to_all(spectra, ('stn', 'beam'), 0, 0, tiled=True)  40.7 us
    all_to_all x1, blocking collectives, body(): owned = lax.all_to_all(formed, ('stn', 'chan', 'beam'), 0, 0, tiled=True)  22.9 us
    pallas_call x1, Pallas kernels, body(): pl.pallas_call(channelize_kernel, grid=(coarse,), out_shape=jax.ShapeDtyp...  7.52 us
    pallas_call x1, Pallas kernels, body(): pl.pallas_call(functools.partial(beam_kernel, amplitude, fine), grid=(coa...  7.51 us
    pallas_call x1, Pallas kernels, body(): pl.pallas_call(order_kernel, grid=(chan,), out_shape=jax.ShapeDtypeStruct...  2.11 us
    ppermute x1, waiting for transfers between devices, body(): other = lax.ppermute(away, 'beam', [(0, 1), (1, 0)])  1.97 us
  transfers between devices with their start and end apart: 1, of which 1 were waited for; matrix products, arithmetic and copies ran while one was open for 0% of the time, Pallas kernels for 0%

profile of v5, /device:TPU:1, one launch (start us, length us, event | category | flops | bytes accessed | tf_op | source)
XLA Modules:
  0.0 85.6 jit_solution(1436994036042672355)
XLA Ops:
  0.0 0.0 copy-start
  0.0 0.0 copy-start.2
  0.0 0.0 copy-start.1
  0.0 1.4 %dynamic-slice_bitcast_fusion = bf16[2,3,16,4608]{3,2,1,0:T(8,128)(2,1)S(1)} fusion(bf16[2,32,3,4608]{3,1,2,0:T(8,128)(2,1)} %param.6, s32[]{:T(128)S(6)} %select_n.3), kind=kLoop, calls=%fused_computation | loop fusion | bytes 1769476 | tf_op jit(solution)/shard_map/dynamic_slice | solution.py:319
  1.4 1.5 %collective-permute-start = (bf16[2,3,16,4608]{3,2,1,0:T(8,128)(2,1)S(1)}, bf16[2,3,16,4608]{3,2,1,0:T(8,128)(2,1)S(1)}, u32[]{:S(2)}, u32[]{:S(2)}) collective-permute-start(bf16[2,3,16,4608]{3,2,1,0:T(8,128)(2,1)S(1)} %dynamic-slice_bitcast_fusion), channel_id=1, source_target_pairs={{0,1},{1,0},{2,3},{3,2},{4,5},{5,4},{6,7},{7,6},{8,9},{9,8},{10,11... | collective-permute-start | bytes 2654216 | tf_op jit(solution)/shard_map/ppermute | solution.py:320
  2.9 0.1 pad_add_fusion.place_ref
  3.0 0.0 copy-done.2
  3.0 2.0 %collective-permute-done.other_ref = bf16[2,3,16,4608]{3,2,1,0:T(8,128)(2,1)S(1)} collective-permute-done((bf16[2,3,16,4608]{3,2,1,0:T(8,128)(2,1)S(1)}, bf16[2,3,16,4608]{3,2,1,0:T(8,128)(2,1)S(1)}, u32[]{:S(2)}, u32[]{:S(2)}) %collective-permute-start) | collective-permute-done | bytes 884768 | tf_op jit(solution)/shard_map/ppermute | solution.py:320
  4.9 0.0 copy-done
  4.9 0.0 copy-done.1
  4.9 7.5 %channelize.1 = bf16[32,13,8,384]{3,2,1,0:T(8,128)(2,1)S(1)} custom-call(s32[1]{0:T(128)} %bitcast.core_ref, s32[32]{0:T(128)S(1)} %copy-done.1, bf16[2,3,32,4608]{3,2,1,0:T(8,128)(2,1)S(1)} %bitcast.10, bf16[2,3,16,4608]{3,2,1,0:T(8,128)(2,1)S(1)} %collective-permute-done.other_ref, f32[16,256]{1,0:T(8,128)} %prototype_ref.1, ...), custom_call_target="tpu_custom_call" | custom-call | tf_op jit(solution)/shard_map/channelize/pallas_call | solution.py:325
  12.5 40.7 %all_to_all.10.code_ref.data_ref = bf16[32,13,8,384]{3,2,1,0:T(8,128)(2,1)S(1)} all-to-all(bf16[32,13,8,384]{3,2,1,0:T(8,128)(2,1)S(1)} %channelize.1), channel_id=1, replica_groups=mesh['stn'=16,'chan'=4,'beam'=2] {'stn','beam'}, dimensions={0} | all-to-all | bytes 5111808 | tf_op jit(solution)/shard_map/all_to_all | solution.py:364
  53.2 7.5 %beamform.1 = bf16[128,3,8,128]{3,2,1,0:T(8,128)(2,1)S(1)} custom-call(s32[2]{0:T(128)S(1)} %pad_add_fusion.place_ref, f32[1,128]{1,0:T(1,128)S(1)} %convert_bitcast_fusion.beam_sub_ref, bf16[32,13,8,384]{3,2,1,0:T(8,128)(2,1)S(1)} %all_to_all.10.code_ref.data_ref, bf16[32,13,8,384]{3,2,1,0:T(8,128)(2,1)S(1)} %all_to_all.10.code_ref.data_ref), custom_call_target="tpu_custom_call" | custom-call | tf_op jit(solution)/shard_map/beamform/pallas_call | solution.py:367
  60.7 22.9 %all_to_all.11 = bf16[128,3,8,128]{3,2,1,0:T(8,128)(2,1)S(1)} all-to-all(bf16[128,3,8,128]{3,2,1,0:T(8,128)(2,1)S(1)} %beamform.1), channel_id=1, replica_groups=mesh['stn'=16,'chan'=4,'beam'=2] {'stn','chan','beam'}, dimensions={0} | all-to-all | bytes 1572864 | tf_op jit(solution)/shard_map/all_to_all | solution.py:389
  83.5 2.1 %order.1 = f32[1,2,12,48,256]{4,3,2,1,0:T(8,128)} custom-call(bf16[16,4,2,3,8,128]{5,4,3,2,1,0:T(8,128)(2,1)S(1)} %bitcast.11), custom_call_target="tpu_custom_call" | custom-call | tf_op jit(solution)/shard_map/order/pallas_call | solution.py:391
  (1 shorter events, 0.0 us)
Async XLA Ops:
  0.0 4.9 %copy-start = (bf16[2,32,3,4608]{3,1,2,0:T(8,128)(2,1)S(1)}, bf16[2,32,3,4608]{3,1,2,0:T(8,128)(2,1)}, u32[]{:S(2)}) copy-start(bf16[2,32,3,4608]{3,1,2,0:T(8,128)(2,1)} %param.6) | copy-start | bytes 5308420
  0.0 3.0 %copy-start.2 = (s32[128]{0:T(128)S(1)}, s32[128]{0:T(128)}, u32[]{:S(2)}) copy-start(s32[128]{0:T(128)} %param.10) | copy-start | bytes 1540
  0.0 4.9 %copy-start.1 = (s32[32]{0:T(128)S(1)}, s32[32]{0:T(128)}, u32[]{:S(2)}) copy-start(s32[32]{0:T(128)} %sub_ref.1) | copy-start | bytes 388
  1.4 3.6 %collective-permute-start = (bf16[2,3,16,4608]{3,2,1,0:T(8,128)(2,1)S(1)}, bf16[2,3,16,4608]{3,2,1,0:T(8,128)(2,1)S(1)}, u32[]{:S(2)}, u32[]{:S(2)}) collective-permute-start(bf16[2,3,16,4608]{3,2,1,0:T(8,128)(2,1)S(1)} %dynamic-slice_bitcast_fusion), channel_id=1, source_target_pairs={{0,1},{1,0},{2,3},{3,2},{4,5},{5,4},{6,7},{7,6},{8,9},{9,8},{10,11... | collective-permute-start | bytes 2654216 | tf_op jit(solution)/shard_map/ppermute | solution.py:320
